TPU v7x, 256 devices: a whole 4x4x8 slice. The times are simulated.
256 devices in a mesh: dp: 16 (over x_lo, z), ctx: 16 (over x_hi, y, core).
Axes of the slice: x: 4 (x_hi: 2, x_lo: 2; x = x_hi * 2 + x_lo), y: 4, z: 8, core: 2. Of those that a mesh axis runs over, the one named last changes fastest.
Arguments:
- queries: bfloat16 [16, 2304, 1024], P('dp', 'ctx'), may hold values from -6 to 6
- keys: bfloat16 [16, 2304, 1024], P('dp', 'ctx'), may hold values from -6 to 6
- values: bfloat16 [16, 2304, 1024], P('dp', 'ctx'), may hold values from -6 to 6
- gates: bfloat16 [16, 2304, 1024], P('dp', 'ctx'), may hold values from -6 to 6
- attn_out: bfloat16 [16, 2304, 1024], P('dp', 'ctx'), may hold values from -6 to 6
- grad_out: bfloat16 [16, 2304, 1024], P('dp', 'ctx'), may hold values from -6 to 6
- route: int32 [16, 256], P('dp', 'ctx'), may hold values from 0 to 15, as said below
- lengths: int32 [16, 4], P('dp'), may hold values from 1 to 1152, 2304 in all within a row
Outputs:
- grad_queries: bfloat16 [16, 2304, 1024], P('dp', 'ctx')
- grad_keys: bfloat16 [16, 2304, 1024], P('dp', 'ctx')
- grad_values: bfloat16 [16, 2304, 1024], P('dp', 'ctx')
- grad_gates: bfloat16 [16, 2304, 1024], P('dp', 'ctx')
Inputs may be any that keep to these rules, and one draw needn't show every extreme that they name: In each row of route, each aligned block of 16 entries starting at a multiple of 16 names every bucket stream once. Each row of lengths sums to 2304, and its largest entry is 1152.
All inputs are finite; a program needn't handle non-finite values.
Results may differ from a plain program's by a relative error of at most 0.0058.
Values may be sent and summed in bfloat16 or wider, within the bound.
A program may use at most 128 MiB of HBM per device.

v0:
```python
import math

import jax
import jax.numpy as jnp
from jax import lax
from jax.sharding import PartitionSpec as P

HEADS = 8
ATT_DIV = 32


def from_behind(array, axis, by):
    length = lax.axis_size(axis)
    return lax.ppermute(array, axis, [(i, (i + by) % length) for i in range(length)])


def attend(q_heads, k_heads, v_heads, do_heads, live_mask, score_scale):
    scores = (
        jnp.einsum("phd,rhd->hpr", q_heads, k_heads, preferred_element_type=jnp.float32)
        * score_scale
    )
    sig_val = jax.nn.sigmoid(scores)
    weight = (live_mask[None] * scores * sig_val / ATT_DIV).astype(jnp.bfloat16)
    dweight = jnp.einsum("phd,rhd->hpr", do_heads, v_heads, preferred_element_type=jnp.float32)
    dscore = (
        live_mask[None] * dweight * sig_val * (1.0 + scores * (1.0 - sig_val)) / ATT_DIV
    ).astype(jnp.bfloat16)
    grad_v = jnp.einsum("hpr,phd->rhd", weight, do_heads, preferred_element_type=jnp.float32)
    grad_q = (
        jnp.einsum("hpr,rhd->phd", dscore, k_heads, preferred_element_type=jnp.float32)
        * score_scale
    )
    grad_k = (
        jnp.einsum("hpr,phd->rhd", dscore, q_heads, preferred_element_type=jnp.float32)
        * score_scale
    )
    return (grad_q, grad_k, grad_v)


def local(queries, keys, values, gates, attn_out, grad_out, route, lengths):
    shard_rows = queries.shape[1]
    feat_dim = queries.shape[2]
    dp_size = lax.axis_size("dp")
    ctx_size = lax.axis_size("ctx")
    block_rows = shard_rows // dp_size
    head_dim = feat_dim // HEADS
    half_rows = shard_rows // 2
    score_scale = 1.0 / math.sqrt(head_dim)
    targets = route[0]
    send_order = jnp.argsort(targets)

    def to_buckets(array):
        return array[0].reshape(dp_size, block_rows, feat_dim)[send_order]

    arrived = (
        lax.all_to_all(to_buckets(queries), "dp", split_axis=0, concat_axis=0, tiled=True),
        lax.all_to_all(to_buckets(keys), "dp", split_axis=0, concat_axis=0, tiled=True),
        lax.all_to_all(to_buckets(values), "dp", split_axis=0, concat_axis=0, tiled=True),
        lax.all_to_all(to_buckets(gates), "dp", split_axis=0, concat_axis=0, tiled=True),
        lax.all_to_all(to_buckets(attn_out), "dp", split_axis=0, concat_axis=0, tiled=True),
        lax.all_to_all(to_buckets(grad_out), "dp", split_axis=0, concat_axis=0, tiled=True),
    )
    q_rows, k_rows, v_rows, u_rows, o_rows, dy_rows = [
        member.reshape(shard_rows, feat_dim) for member in arrived
    ]
    o_full = o_rows.astype(jnp.float32)
    row_mean = jnp.mean(o_full, axis=1, keepdims=True)
    centred = o_full - row_mean
    inv_std = 1.0 / jnp.sqrt(jnp.mean(centred * centred, axis=1, keepdims=True) + 1e-05)
    normed = centred * inv_std
    dy_full = dy_rows.astype(jnp.float32)
    grad_u = (dy_full * normed).astype(jnp.bfloat16)
    g_term = dy_full * u_rows.astype(jnp.float32)
    d_o = (
        inv_std
        * (
            g_term
            - jnp.mean(g_term, axis=1, keepdims=True)
            - normed * jnp.mean(g_term * normed, axis=1, keepdims=True)
        )
    ).astype(jnp.bfloat16)
    ctx_index = lax.axis_index("ctx")
    user_ends = jnp.cumsum(lengths[0])

    def place_of(rows):
        shard = rows // shard_rows
        inner = rows % shard_rows
        early = shard * half_rows + inner
        late = (2 * ctx_size - 1 - shard) * half_rows + inner - half_rows
        return jnp.where(inner < half_rows, early, late)

    def segment_of(positions):
        return jnp.sum((positions[:, None] >= user_ends[None, :]).astype(jnp.int32), axis=1)

    query_pos = place_of(ctx_index * shard_rows + jnp.arange(shard_rows, dtype=jnp.int32))
    query_seg = segment_of(query_pos)

    def key_block(q_heads, k_heads, v_heads, do_heads, key_start):
        key_pos = place_of(key_start + jnp.arange(k_heads.shape[0], dtype=jnp.int32))
        live_mask = (
            (query_seg[:, None] == segment_of(key_pos)[None, :])
            & (key_pos[None, :] <= query_pos[:, None])
        ).astype(jnp.float32)
        return attend(q_heads, k_heads, v_heads, do_heads, live_mask, score_scale)

    q_heads = q_rows.reshape(shard_rows, HEADS, head_dim)
    k_heads = k_rows.reshape(shard_rows, HEADS, head_dim)
    v_heads = v_rows.reshape(shard_rows, HEADS, head_dim)
    do_heads = d_o.reshape(shard_rows, HEADS, head_dim)
    zero_heads = jnp.zeros((shard_rows, HEADS, head_dim), jnp.float32)

    def cycle_step(cycle_turn, state):
        k_now, v_now, dk_now, dv_now, dq_sum = state
        key_index = (ctx_index - cycle_turn) % ctx_size
        grad_q, grad_k, grad_v = key_block(q_heads, k_now, v_now, do_heads, key_index * shard_rows)
        k_next, v_next = from_behind((k_now, v_now), "ctx", 1)
        dk_next, dv_next = from_behind((dk_now + grad_k, dv_now + grad_v), "ctx", 1)
        return (k_next, v_next, dk_next, dv_next, dq_sum + grad_q)

    final = lax.fori_loop(
        0, ctx_size, cycle_step, (k_heads, v_heads, zero_heads, zero_heads, zero_heads)
    )
    dq_total, dk_total, dv_total = (final[4], final[2], final[3])

    def to_sources(array):
        return array.reshape(dp_size, block_rows, feat_dim).astype(jnp.bfloat16)

    home = (
        lax.all_to_all(to_sources(dq_total), "dp", split_axis=0, concat_axis=0, tiled=True),
        lax.all_to_all(to_sources(dk_total), "dp", split_axis=0, concat_axis=0, tiled=True),
        lax.all_to_all(to_sources(dv_total), "dp", split_axis=0, concat_axis=0, tiled=True),
        lax.all_to_all(to_sources(grad_u), "dp", split_axis=0, concat_axis=0, tiled=True),
    )
    return tuple((member[targets].reshape(1, shard_rows, feat_dim) for member in home))


def solution(mesh):
    in_specs = (
        P("dp", "ctx", None),
        P("dp", "ctx", None),
        P("dp", "ctx", None),
        P("dp", "ctx", None),
        P("dp", "ctx", None),
        P("dp", "ctx", None),
        P("dp", "ctx"),
        P("dp", None),
    )
    out_specs = (
        P("dp", "ctx", None),
        P("dp", "ctx", None),
        P("dp", "ctx", None),
        P("dp", "ctx", None),
    )
    return jax.shard_map(local, mesh=mesh, in_specs=in_specs, out_specs=out_specs, check_vma=False)
```

profile of v0, /device:TPU:24, one launch (start us, length us, event | category | flops | bytes accessed | tf_op | source)
XLA Modules:
  0.0 663.0 jit_solution(14600852589449303406)
XLA Ops:
  5.0 9.5 %all-to-all-start.2 = ((bf16[16,9,1024]{2,1,0:T(8,128)(2,1)}), bf16[16,9,1024]{2,1,0:T(8,128)(2,1)S(1)}, u32[]{:S(2)}, u32[]{:S(2)}) async-start(bf16[16,9,1024]{2,1,0:T(8,128)(2,1)} %gather_fusion.2), calls=%async_computation.2 | async-start | bytes 1048576 | tf_op jit(solution)/shard_map/all_to_all | solution.py:60
  16.1 14.2 %all-to-all-done.2 = bf16[16,9,1024]{2,1,0:T(8,128)(2,1)S(1)} async-done(((bf16[16,9,1024]{2,1,0:T(8,128)(2,1)}), bf16[16,9,1024]{2,1,0:T(8,128)(2,1)S(1)}, u32[]{:S(2)}, u32[]{:S(2)}) %all-to-all-start.2) | async-done | bytes 294944 | tf_op jit(solution)/shard_map/all_to_all | solution.py:60
  36.3 13.0 %all-to-all-done.3 = bf16[16,9,1024]{2,1,0:T(8,128)(2,1)S(1)} async-done(((bf16[16,9,1024]{2,1,0:T(8,128)(2,1)}), bf16[16,9,1024]{2,1,0:T(8,128)(2,1)S(1)}, u32[]{:S(2)}, u32[]{:S(2)}) %all-to-all-start.3) | async-done | bytes 294944 | tf_op jit(solution)/shard_map/all_to_all | solution.py:61
  56.0 12.3 %all-to-all-done.4 = bf16[16,9,1024]{2,1,0:T(8,128)(2,1)S(1)} async-done(((bf16[16,9,1024]{2,1,0:T(8,128)(2,1)}), bf16[16,9,1024]{2,1,0:T(8,128)(2,1)S(1)}, u32[]{:S(2)}, u32[]{:S(2)}) %all-to-all-start.4) | async-done | bytes 294944 | tf_op jit(solution)/shard_map/all_to_all | solution.py:59
  77.0 10.4 %all-to-all-done = bf16[16,9,1024]{2,1,0:T(8,128)(2,1)S(1)} async-done(((bf16[16,9,1024]{2,1,0:T(8,128)(2,1)}), bf16[16,9,1024]{2,1,0:T(8,128)(2,1)S(1)}, u32[]{:S(2)}, u32[]{:S(2)}) %all-to-all-start) | async-done | bytes 294944 | tf_op jit(solution)/shard_map/all_to_all | solution.py:57
  92.9 13.6 %all-to-all-done.1 = bf16[16,9,1024]{2,1,0:T(8,128)(2,1)S(1)} async-done(((bf16[16,9,1024]{2,1,0:T(8,128)(2,1)}), bf16[16,9,1024]{2,1,0:T(8,128)(2,1)S(1)}, u32[]{:S(2)}, u32[]{:S(2)}) %all-to-all-start.1) | async-done | bytes 294944 | tf_op jit(solution)/shard_map/all_to_all | solution.py:58
  116.7 9.8 %all-to-all-done.5 = bf16[16,9,1024]{2,1,0:T(8,128)(2,1)} async-done(((bf16[16,9,1024]{2,1,0:T(8,128)(2,1)}), bf16[16,9,1024]{2,1,0:T(8,128)(2,1)}, u32[]{:S(2)}, u32[]{:S(2)}) %all-to-all-start.5) | async-done | bytes 294944 | tf_op jit(solution)/shard_map/all_to_all | solution.py:56
  128.6 455.4 %while.25 = (s32[]{:T(128)}, bf16[144,8,128]{2,0,1:T(8,128)(2,1)S(1)}, bf16[144,8,128]{2,0,1:T(8,128)(2,1)S(1)}, f32[144,8,128]{2,0,1:T(8,128)S(1)}, f32[144,8,1...) while((s32[]{:T(128)}, ...), condition=%wide.region_9.10_spmd.clone, body=%wide.region_7.9_spmd.clone.sunk | while | flops 216712656 | bytes 17186020 | solution.py:120
  139.4 11.6 %collective-permute-done = bf16[144,8,128]{2,0,1:T(8,128)(2,1)S(1)} collective-permute-done((bf16[144,8,128]{2,0,1:T(8,128)(2,1)S(1)}, bf16[144,8,128]{2,0,1:T(8,128)(2,1)S(1)}, u32[]{:S(2)}, u32[]{:S(2)}) %collective-permute-start) | collective-permute-done | bytes 294944 | tf_op jit(solution)/shard_map/while/body/eval_jaxpr/ppermute | solution.py:14
  166.9 9.6 %collective-permute-done = bf16[144,8,128]{2,0,1:T(8,128)(2,1)S(1)} collective-permute-done((bf16[144,8,128]{2,0,1:T(8,128)(2,1)S(1)}, bf16[144,8,128]{2,0,1:T(8,128)(2,1)S(1)}, u32[]{:S(2)}, u32[]{:S(2)}) %collective-permute-start) | collective-permute-done | bytes 294944 | tf_op jit(solution)/shard_map/while/body/eval_jaxpr/ppermute | solution.py:14
  196.0 6.3 collective-permute-done
  209.0 7.1 %collective-permute-start.2 = (f32[144,8,128]{2,0,1:T(8,128)S(1)}, f32[144,8,128]{2,0,1:T(8,128)S(1)}, u32[]{:S(2)}, u32[]{:S(2)}) collective-permute-start(f32[144,8,128]{2,0,1:T(8,128)S(1)} %fusion.61), channel_id=1, source_target_pairs={{0,1},{1,2},{2,3},{3,4},{4,5},{5,6},{6,7},{7,8},{8,9},{9,10},{10,1... | collective-permute-start | bytes 1769480 | tf_op jit(solution)/shard_map/while/body/eval_jaxpr/ppermute | solution.py:14
  218.8 6.0 collective-permute-start.3
  225.1 6.3 collective-permute-done
  238.1 7.1 %collective-permute-start.2 = (f32[144,8,128]{2,0,1:T(8,128)S(1)}, f32[144,8,128]{2,0,1:T(8,128)S(1)}, u32[]{:S(2)}, u32[]{:S(2)}) collective-permute-start(f32[144,8,128]{2,0,1:T(8,128)S(1)} %fusion.61), channel_id=1, source_target_pairs={{0,1},{1,2},{2,3},{3,4},{4,5},{5,6},{6,7},{7,8},{8,9},{9,10},{10,1... | collective-permute-start | bytes 1769480 | tf_op jit(solution)/shard_map/while/body/eval_jaxpr/ppermute | solution.py:14
  247.9 6.0 collective-permute-start.3
  254.2 6.3 collective-permute-done
  267.2 7.1 %collective-permute-start.2 = (f32[144,8,128]{2,0,1:T(8,128)S(1)}, f32[144,8,128]{2,0,1:T(8,128)S(1)}, u32[]{:S(2)}, u32[]{:S(2)}) collective-permute-start(f32[144,8,128]{2,0,1:T(8,128)S(1)} %fusion.61), channel_id=1, source_target_pairs={{0,1},{1,2},{2,3},{3,4},{4,5},{5,6},{6,7},{7,8},{8,9},{9,10},{10,1... | collective-permute-start | bytes 1769480 | tf_op jit(solution)/shard_map/while/body/eval_jaxpr/ppermute | solution.py:14
  277.0 6.0 collective-permute-start.3
  283.4 6.3 collective-permute-done
  296.3 7.1 %collective-permute-start.2 = (f32[144,8,128]{2,0,1:T(8,128)S(1)}, f32[144,8,128]{2,0,1:T(8,128)S(1)}, u32[]{:S(2)}, u32[]{:S(2)}) collective-permute-start(f32[144,8,128]{2,0,1:T(8,128)S(1)} %fusion.61), channel_id=1, source_target_pairs={{0,1},{1,2},{2,3},{3,4},{4,5},{5,6},{6,7},{7,8},{8,9},{9,10},{10,1... | collective-permute-start | bytes 1769480 | tf_op jit(solution)/shard_map/while/body/eval_jaxpr/ppermute | solution.py:14
  306.1 6.0 collective-permute-start.3
  312.5 6.3 collective-permute-done
  325.4 7.1 %collective-permute-start.2 = (f32[144,8,128]{2,0,1:T(8,128)S(1)}, f32[144,8,128]{2,0,1:T(8,128)S(1)}, u32[]{:S(2)}, u32[]{:S(2)}) collective-permute-start(f32[144,8,128]{2,0,1:T(8,128)S(1)} %fusion.61), channel_id=1, source_target_pairs={{0,1},{1,2},{2,3},{3,4},{4,5},{5,6},{6,7},{7,8},{8,9},{9,10},{10,1... | collective-permute-start | bytes 1769480 | tf_op jit(solution)/shard_map/while/body/eval_jaxpr/ppermute | solution.py:14
  335.2 6.0 collective-permute-start.3
  341.6 6.3 collective-permute-done
  354.5 7.1 %collective-permute-start.2 = (f32[144,8,128]{2,0,1:T(8,128)S(1)}, f32[144,8,128]{2,0,1:T(8,128)S(1)}, u32[]{:S(2)}, u32[]{:S(2)}) collective-permute-start(f32[144,8,128]{2,0,1:T(8,128)S(1)} %fusion.61), channel_id=1, source_target_pairs={{0,1},{1,2},{2,3},{3,4},{4,5},{5,6},{6,7},{7,8},{8,9},{9,10},{10,1... | collective-permute-start | bytes 1769480 | tf_op jit(solution)/shard_map/while/body/eval_jaxpr/ppermute | solution.py:14
  364.4 6.0 collective-permute-start.3
  370.7 6.3 collective-permute-done
  383.7 7.1 %collective-permute-start.2 = (f32[144,8,128]{2,0,1:T(8,128)S(1)}, f32[144,8,128]{2,0,1:T(8,128)S(1)}, u32[]{:S(2)}, u32[]{:S(2)}) collective-permute-start(f32[144,8,128]{2,0,1:T(8,128)S(1)} %fusion.61), channel_id=1, source_target_pairs={{0,1},{1,2},{2,3},{3,4},{4,5},{5,6},{6,7},{7,8},{8,9},{9,10},{10,1... | collective-permute-start | bytes 1769480 | tf_op jit(solution)/shard_map/while/body/eval_jaxpr/ppermute | solution.py:14
  399.8 6.3 collective-permute-done
  412.8 7.1 %collective-permute-start.2 = (f32[144,8,128]{2,0,1:T(8,128)S(1)}, f32[144,8,128]{2,0,1:T(8,128)S(1)}, u32[]{:S(2)}, u32[]{:S(2)}) collective-permute-start(f32[144,8,128]{2,0,1:T(8,128)S(1)} %fusion.61), channel_id=1, source_target_pairs={{0,1},{1,2},{2,3},{3,4},{4,5},{5,6},{6,7},{7,8},{8,9},{9,10},{10,1... | collective-permute-start | bytes 1769480 | tf_op jit(solution)/shard_map/while/body/eval_jaxpr/ppermute | solution.py:14
  429.0 6.3 collective-permute-done
  441.9 7.1 %collective-permute-start.2 = (f32[144,8,128]{2,0,1:T(8,128)S(1)}, f32[144,8,128]{2,0,1:T(8,128)S(1)}, u32[]{:S(2)}, u32[]{:S(2)}) collective-permute-start(f32[144,8,128]{2,0,1:T(8,128)S(1)} %fusion.61), channel_id=1, source_target_pairs={{0,1},{1,2},{2,3},{3,4},{4,5},{5,6},{6,7},{7,8},{8,9},{9,10},{10,1... | collective-permute-start | bytes 1769480 | tf_op jit(solution)/shard_map/while/body/eval_jaxpr/ppermute | solution.py:14
  458.1 6.3 collective-permute-done
  471.0 7.1 %collective-permute-start.2 = (f32[144,8,128]{2,0,1:T(8,128)S(1)}, f32[144,8,128]{2,0,1:T(8,128)S(1)}, u32[]{:S(2)}, u32[]{:S(2)}) collective-permute-start(f32[144,8,128]{2,0,1:T(8,128)S(1)} %fusion.61), channel_id=1, source_target_pairs={{0,1},{1,2},{2,3},{3,4},{4,5},{5,6},{6,7},{7,8},{8,9},{9,10},{10,1... | collective-permute-start | bytes 1769480 | tf_op jit(solution)/shard_map/while/body/eval_jaxpr/ppermute | solution.py:14
  487.2 6.3 collective-permute-done
  500.1 7.1 %collective-permute-start.2 = (f32[144,8,128]{2,0,1:T(8,128)S(1)}, f32[144,8,128]{2,0,1:T(8,128)S(1)}, u32[]{:S(2)}, u32[]{:S(2)}) collective-permute-start(f32[144,8,128]{2,0,1:T(8,128)S(1)} %fusion.61), channel_id=1, source_target_pairs={{0,1},{1,2},{2,3},{3,4},{4,5},{5,6},{6,7},{7,8},{8,9},{9,10},{10,1... | collective-permute-start | bytes 1769480 | tf_op jit(solution)/shard_map/while/body/eval_jaxpr/ppermute | solution.py:14
  516.3 6.3 collective-permute-done
  529.3 7.1 %collective-permute-start.2 = (f32[144,8,128]{2,0,1:T(8,128)S(1)}, f32[144,8,128]{2,0,1:T(8,128)S(1)}, u32[]{:S(2)}, u32[]{:S(2)}) collective-permute-start(f32[144,8,128]{2,0,1:T(8,128)S(1)} %fusion.61), channel_id=1, source_target_pairs={{0,1},{1,2},{2,3},{3,4},{4,5},{5,6},{6,7},{7,8},{8,9},{9,10},{10,1... | collective-permute-start | bytes 1769480 | tf_op jit(solution)/shard_map/while/body/eval_jaxpr/ppermute | solution.py:14
  545.4 6.3 collective-permute-done
  558.4 7.1 %collective-permute-start.2 = (f32[144,8,128]{2,0,1:T(8,128)S(1)}, f32[144,8,128]{2,0,1:T(8,128)S(1)}, u32[]{:S(2)}, u32[]{:S(2)}) collective-permute-start(f32[144,8,128]{2,0,1:T(8,128)S(1)} %fusion.61), channel_id=1, source_target_pairs={{0,1},{1,2},{2,3},{3,4},{4,5},{5,6},{6,7},{7,8},{8,9},{9,10},{10,1... | collective-permute-start | bytes 1769480 | tf_op jit(solution)/shard_map/while/body/eval_jaxpr/ppermute | solution.py:14
  574.6 6.3 collective-permute-done
  590.8 10.5 %all-to-all-done.6 = bf16[16,9,1024]{2,1,0:T(8,128)(2,1)S(1)} async-done(((bf16[16,9,1024]{2,1,0:T(8,128)(2,1)}), bf16[16,9,1024]{2,1,0:T(8,128)(2,1)S(1)}, u32[]{:S(2)}, u32[]{:S(2)}) %all-to-all-start.6) | async-done | bytes 294944 | tf_op jit(solution)/shard_map/all_to_all | solution.py:129
  607.1 11.2 %all-to-all-done.7 = bf16[16,9,1024]{2,1,0:T(8,128)(2,1)S(1)} async-done(((bf16[16,9,1024]{2,1,0:T(8,128)(2,1)}), bf16[16,9,1024]{2,1,0:T(8,128)(2,1)S(1)}, u32[]{:S(2)}, u32[]{:S(2)}) %all-to-all-start.7) | async-done | bytes 294944 | tf_op jit(solution)/shard_map/all_to_all | solution.py:130
  618.3 20.6 %all_to_all.50 = bf16[16,9,1024]{2,1,0:T(8,128)(2,1)S(1)} all-to-all(bf16[16,9,1024]{2,1,0:T(8,128)(2,1)S(1)} %convert_element_type.117), channel_id=1, replica_groups=mesh['dp'=16,'ctx'=16] {'dp'}, dimensions={0} | all-to-all | bytes 589824 | tf_op jit(solution)/shard_map/all_to_all | solution.py:131
  638.9 6.9 %all-to-all-start.9 = ((bf16[16,9,1024]{2,1,0:T(8,128)(2,1)}), bf16[16,9,1024]{2,1,0:T(8,128)(2,1)S(1)}, u32[]{:S(2)}, u32[]{:S(2)}) async-start(bf16[16,9,1024]{2,1,0:T(8,128)(2,1)} %get-tuple-element.434), calls=%async_computation.9 | async-start | bytes 1048576 | tf_op jit(solution)/shard_map/all_to_all | solution.py:132
  650.1 11.5 %all-to-all-done.9 = bf16[16,9,1024]{2,1,0:T(8,128)(2,1)S(1)} async-done(((bf16[16,9,1024]{2,1,0:T(8,128)(2,1)}), bf16[16,9,1024]{2,1,0:T(8,128)(2,1)S(1)}, u32[]{:S(2)}, u32[]{:S(2)}) %all-to-all-start.9) | async-done | bytes 294944 | tf_op jit(solution)/shard_map/all_to_all | solution.py:132
  (375 shorter events, 279.7 us)
Async XLA Ops:
  5.0 25.2 %all-to-all-start.2 = ((bf16[16,9,1024]{2,1,0:T(8,128)(2,1)}), bf16[16,9,1024]{2,1,0:T(8,128)(2,1)S(1)}, u32[]{:S(2)}, u32[]{:S(2)}) async-start(bf16[16,9,1024]{2,1,0:T(8,128)(2,1)} %gather_fusion.2), calls=%async_computation.2 | async-start | bytes 1048576 | tf_op jit(solution)/shard_map/all_to_all | solution.py:60
  30.2 19.1 %all-to-all-start.3 = ((bf16[16,9,1024]{2,1,0:T(8,128)(2,1)}), bf16[16,9,1024]{2,1,0:T(8,128)(2,1)S(1)}, u32[]{:S(2)}, u32[]{:S(2)}) async-start(bf16[16,9,1024]{2,1,0:T(8,128)(2,1)} %gather_fusion.3), calls=%async_computation.3 | async-start | bytes 1048576 | tf_op jit(solution)/shard_map/all_to_all | solution.py:61
  49.3 19.0 %all-to-all-start.4 = ((bf16[16,9,1024]{2,1,0:T(8,128)(2,1)}), bf16[16,9,1024]{2,1,0:T(8,128)(2,1)S(1)}, u32[]{:S(2)}, u32[]{:S(2)}) async-start(bf16[16,9,1024]{2,1,0:T(8,128)(2,1)} %gather_fusion.4), calls=%async_computation.4 | async-start | bytes 1048576 | tf_op jit(solution)/shard_map/all_to_all | solution.py:59
  68.4 19.1 %all-to-all-start = ((bf16[16,9,1024]{2,1,0:T(8,128)(2,1)}), bf16[16,9,1024]{2,1,0:T(8,128)(2,1)S(1)}, u32[]{:S(2)}, u32[]{:S(2)}) async-start(bf16[16,9,1024]{2,1,0:T(8,128)(2,1)} %gather_fusion), calls=%async_computation | async-start | bytes 1048576 | tf_op jit(solution)/shard_map/all_to_all | solution.py:57
  87.4 19.1 %all-to-all-start.1 = ((bf16[16,9,1024]{2,1,0:T(8,128)(2,1)}), bf16[16,9,1024]{2,1,0:T(8,128)(2,1)S(1)}, u32[]{:S(2)}, u32[]{:S(2)}) async-start(bf16[16,9,1024]{2,1,0:T(8,128)(2,1)} %gather_fusion.1), calls=%async_computation.1 | async-start | bytes 1048576 | tf_op jit(solution)/shard_map/all_to_all | solution.py:58
  107.3 19.2 %all-to-all-start.5 = ((bf16[16,9,1024]{2,1,0:T(8,128)(2,1)}), bf16[16,9,1024]{2,1,0:T(8,128)(2,1)}, u32[]{:S(2)}, u32[]{:S(2)}) async-start(bf16[16,9,1024]{2,1,0:T(8,128)(2,1)} %gather_fusion.5), calls=%async_computation.5 | async-start | bytes 1048576 | tf_op jit(solution)/shard_map/all_to_all | solution.py:56
  132.1 22.0 %collective-permute-start.2 = (f32[144,8,128]{2,0,1:T(8,128)S(1)}, f32[144,8,128]{2,0,1:T(8,128)S(1)}, u32[]{:S(2)}, u32[]{:S(2)}) collective-permute-start(f32[144,8,128]{2,0,1:T(8,128)S(1)} %fusion.61), channel_id=1, source_target_pairs={{0,1},{1,2},{2,3},{3,4},{4,5},{5,6},{6,7},{7,8},{8,9},{9,10},{10,1... | collective-permute-start | bytes 1769480 | tf_op jit(solution)/shard_map/while/body/eval_jaxpr/ppermute | solution.py:14
  134.9 19.2 %collective-permute-start.3 = (f32[144,8,128]{2,0,1:T(8,128)}, f32[144,8,128]{2,0,1:T(8,128)}, u32[]{:S(2)}, u32[]{:S(2)}) collective-permute-start(f32[144,8,128]{2,0,1:T(8,128)} %fusion.63), channel_id=1, source_target_pairs={{0,1},{1,2},{2,3},{3,4},{4,5},{5,6},{6,7},{7,8},{8,9},{9,10},{10,1... | collective-permute-start | bytes 1769480 | tf_op jit(solution)/shard_map/while/body/eval_jaxpr/ppermute | solution.py:14
  137.4 13.6 %collective-permute-start = (bf16[144,8,128]{2,0,1:T(8,128)(2,1)S(1)}, bf16[144,8,128]{2,0,1:T(8,128)(2,1)S(1)}, u32[]{:S(2)}, u32[]{:S(2)}) collective-permute-start(bf16[144,8,128]{2,0,1:T(8,128)(2,1)S(1)} %copy.41), channel_id=1, source_target_pairs={{0,1},{1,2},{2,3},{3,4},{4,5},{5,6},{6,7},{7,8},{8,9},{9,10},{10,1... | collective-permute-start | bytes 884744 | tf_op jit(solution)/shard_map/while/body/eval_jaxpr/ppermute | solution.py:14
  137.4 16.7 %collective-permute-start.1 = (bf16[144,8,128]{2,0,1:T(8,128)(2,1)}, bf16[144,8,128]{2,0,1:T(8,128)(2,1)S(1)}, u32[]{:S(2)}, u32[]{:S(2)}) collective-permute-start(bf16[144,8,128]{2,0,1:T(8,128)(2,1)} %copy.42), channel_id=1, source_target_pairs={{0,1},{1,2},{2,3},{3,4},{4,5},{5,6},{6,7},{7,8},{8,9},{9,10},{10,1... | collective-permute-start | bytes 884744 | tf_op jit(solution)/shard_map/while/body/eval_jaxpr/ppermute | solution.py:14
  157.6 22.0 %collective-permute-start.2 = (f32[144,8,128]{2,0,1:T(8,128)S(1)}, f32[144,8,128]{2,0,1:T(8,128)S(1)}, u32[]{:S(2)}, u32[]{:S(2)}) collective-permute-start(f32[144,8,128]{2,0,1:T(8,128)S(1)} %fusion.61), channel_id=1, source_target_pairs={{0,1},{1,2},{2,3},{3,4},{4,5},{5,6},{6,7},{7,8},{8,9},{9,10},{10,1... | collective-permute-start | bytes 1769480 | tf_op jit(solution)/shard_map/while/body/eval_jaxpr/ppermute | solution.py:14
  160.5 19.1 %collective-permute-start.3 = (f32[144,8,128]{2,0,1:T(8,128)}, f32[144,8,128]{2,0,1:T(8,128)}, u32[]{:S(2)}, u32[]{:S(2)}) collective-permute-start(f32[144,8,128]{2,0,1:T(8,128)} %fusion.63), channel_id=1, source_target_pairs={{0,1},{1,2},{2,3},{3,4},{4,5},{5,6},{6,7},{7,8},{8,9},{9,10},{10,1... | collective-permute-start | bytes 1769480 | tf_op jit(solution)/shard_map/while/body/eval_jaxpr/ppermute | solution.py:14
  166.5 10.0 %collective-permute-start = (bf16[144,8,128]{2,0,1:T(8,128)(2,1)S(1)}, bf16[144,8,128]{2,0,1:T(8,128)(2,1)S(1)}, u32[]{:S(2)}, u32[]{:S(2)}) collective-permute-start(bf16[144,8,128]{2,0,1:T(8,128)(2,1)S(1)} %copy.41), channel_id=1, source_target_pairs={{0,1},{1,2},{2,3},{3,4},{4,5},{5,6},{6,7},{7,8},{8,9},{9,10},{10,1... | collective-permute-start | bytes 884744 | tf_op jit(solution)/shard_map/while/body/eval_jaxpr/ppermute | solution.py:14
  166.5 13.1 %collective-permute-start.1 = (bf16[144,8,128]{2,0,1:T(8,128)(2,1)}, bf16[144,8,128]{2,0,1:T(8,128)(2,1)S(1)}, u32[]{:S(2)}, u32[]{:S(2)}) collective-permute-start(bf16[144,8,128]{2,0,1:T(8,128)(2,1)} %copy.42), channel_id=1, source_target_pairs={{0,1},{1,2},{2,3},{3,4},{4,5},{5,6},{6,7},{7,8},{8,9},{9,10},{10,1... | collective-permute-start | bytes 884744 | tf_op jit(solution)/shard_map/while/body/eval_jaxpr/ppermute | solution.py:14
  183.1 22.4 %collective-permute-start.2 = (f32[144,8,128]{2,0,1:T(8,128)S(1)}, f32[144,8,128]{2,0,1:T(8,128)S(1)}, u32[]{:S(2)}, u32[]{:S(2)}) collective-permute-start(f32[144,8,128]{2,0,1:T(8,128)S(1)} %fusion.61), channel_id=1, source_target_pairs={{0,1},{1,2},{2,3},{3,4},{4,5},{5,6},{6,7},{7,8},{8,9},{9,10},{10,1... | collective-permute-start | bytes 1769480 | tf_op jit(solution)/shard_map/while/body/eval_jaxpr/ppermute | solution.py:14
  189.6 15.8 %collective-permute-start.3 = (f32[144,8,128]{2,0,1:T(8,128)}, f32[144,8,128]{2,0,1:T(8,128)}, u32[]{:S(2)}, u32[]{:S(2)}) collective-permute-start(f32[144,8,128]{2,0,1:T(8,128)} %fusion.63), channel_id=1, source_target_pairs={{0,1},{1,2},{2,3},{3,4},{4,5},{5,6},{6,7},{7,8},{8,9},{9,10},{10,1... | collective-permute-start | bytes 1769480 | tf_op jit(solution)/shard_map/while/body/eval_jaxpr/ppermute | solution.py:14
  195.6 9.8 %collective-permute-start.1 = (bf16[144,8,128]{2,0,1:T(8,128)(2,1)}, bf16[144,8,128]{2,0,1:T(8,128)(2,1)S(1)}, u32[]{:S(2)}, u32[]{:S(2)}) collective-permute-start(bf16[144,8,128]{2,0,1:T(8,128)(2,1)} %copy.42), channel_id=1, source_target_pairs={{0,1},{1,2},{2,3},{3,4},{4,5},{5,6},{6,7},{7,8},{8,9},{9,10},{10,1... | collective-permute-start | bytes 884744 | tf_op jit(solution)/shard_map/while/body/eval_jaxpr/ppermute | solution.py:14
  209.0 25.6 %collective-permute-start.2 = (f32[144,8,128]{2,0,1:T(8,128)S(1)}, f32[144,8,128]{2,0,1:T(8,128)S(1)}, u32[]{:S(2)}, u32[]{:S(2)}) collective-permute-start(f32[144,8,128]{2,0,1:T(8,128)S(1)} %fusion.61), channel_id=1, source_target_pairs={{0,1},{1,2},{2,3},{3,4},{4,5},{5,6},{6,7},{7,8},{8,9},{9,10},{10,1... | collective-permute-start | bytes 1769480 | tf_op jit(solution)/shard_map/while/body/eval_jaxpr/ppermute | solution.py:14
  218.8 15.8 %collective-permute-start.3 = (f32[144,8,128]{2,0,1:T(8,128)}, f32[144,8,128]{2,0,1:T(8,128)}, u32[]{:S(2)}, u32[]{:S(2)}) collective-permute-start(f32[144,8,128]{2,0,1:T(8,128)} %fusion.63), channel_id=1, source_target_pairs={{0,1},{1,2},{2,3},{3,4},{4,5},{5,6},{6,7},{7,8},{8,9},{9,10},{10,1... | collective-permute-start | bytes 1769480 | tf_op jit(solution)/shard_map/while/body/eval_jaxpr/ppermute | solution.py:14
  224.8 9.8 %collective-permute-start.1 = (bf16[144,8,128]{2,0,1:T(8,128)(2,1)}, bf16[144,8,128]{2,0,1:T(8,128)(2,1)S(1)}, u32[]{:S(2)}, u32[]{:S(2)}) collective-permute-start(bf16[144,8,128]{2,0,1:T(8,128)(2,1)} %copy.42), channel_id=1, source_target_pairs={{0,1},{1,2},{2,3},{3,4},{4,5},{5,6},{6,7},{7,8},{8,9},{9,10},{10,1... | collective-permute-start | bytes 884744 | tf_op jit(solution)/shard_map/while/body/eval_jaxpr/ppermute | solution.py:14
  238.1 25.6 %collective-permute-start.2 = (f32[144,8,128]{2,0,1:T(8,128)S(1)}, f32[144,8,128]{2,0,1:T(8,128)S(1)}, u32[]{:S(2)}, u32[]{:S(2)}) collective-permute-start(f32[144,8,128]{2,0,1:T(8,128)S(1)} %fusion.61), channel_id=1, source_target_pairs={{0,1},{1,2},{2,3},{3,4},{4,5},{5,6},{6,7},{7,8},{8,9},{9,10},{10,1... | collective-permute-start | bytes 1769480 | tf_op jit(solution)/shard_map/while/body/eval_jaxpr/ppermute | solution.py:14
  247.9 15.8 %collective-permute-start.3 = (f32[144,8,128]{2,0,1:T(8,128)}, f32[144,8,128]{2,0,1:T(8,128)}, u32[]{:S(2)}, u32[]{:S(2)}) collective-permute-start(f32[144,8,128]{2,0,1:T(8,128)} %fusion.63), channel_id=1, source_target_pairs={{0,1},{1,2},{2,3},{3,4},{4,5},{5,6},{6,7},{7,8},{8,9},{9,10},{10,1... | collective-permute-start | bytes 1769480 | tf_op jit(solution)/shard_map/while/body/eval_jaxpr/ppermute | solution.py:14
  253.9 9.8 %collective-permute-start.1 = (bf16[144,8,128]{2,0,1:T(8,128)(2,1)}, bf16[144,8,128]{2,0,1:T(8,128)(2,1)S(1)}, u32[]{:S(2)}, u32[]{:S(2)}) collective-permute-start(bf16[144,8,128]{2,0,1:T(8,128)(2,1)} %copy.42), channel_id=1, source_target_pairs={{0,1},{1,2},{2,3},{3,4},{4,5},{5,6},{6,7},{7,8},{8,9},{9,10},{10,1... | collective-permute-start | bytes 884744 | tf_op jit(solution)/shard_map/while/body/eval_jaxpr/ppermute | solution.py:14
  267.2 25.6 %collective-permute-start.2 = (f32[144,8,128]{2,0,1:T(8,128)S(1)}, f32[144,8,128]{2,0,1:T(8,128)S(1)}, u32[]{:S(2)}, u32[]{:S(2)}) collective-permute-start(f32[144,8,128]{2,0,1:T(8,128)S(1)} %fusion.61), channel_id=1, source_target_pairs={{0,1},{1,2},{2,3},{3,4},{4,5},{5,6},{6,7},{7,8},{8,9},{9,10},{10,1... | collective-permute-start | bytes 1769480 | tf_op jit(solution)/shard_map/while/body/eval_jaxpr/ppermute | solution.py:14
  277.0 15.8 %collective-permute-start.3 = (f32[144,8,128]{2,0,1:T(8,128)}, f32[144,8,128]{2,0,1:T(8,128)}, u32[]{:S(2)}, u32[]{:S(2)}) collective-permute-start(f32[144,8,128]{2,0,1:T(8,128)} %fusion.63), channel_id=1, source_target_pairs={{0,1},{1,2},{2,3},{3,4},{4,5},{5,6},{6,7},{7,8},{8,9},{9,10},{10,1... | collective-permute-start | bytes 1769480 | tf_op jit(solution)/shard_map/while/body/eval_jaxpr/ppermute | solution.py:14
  296.3 25.6 %collective-permute-start.2 = (f32[144,8,128]{2,0,1:T(8,128)S(1)}, f32[144,8,128]{2,0,1:T(8,128)S(1)}, u32[]{:S(2)}, u32[]{:S(2)}) collective-permute-start(f32[144,8,128]{2,0,1:T(8,128)S(1)} %fusion.61), channel_id=1, source_target_pairs={{0,1},{1,2},{2,3},{3,4},{4,5},{5,6},{6,7},{7,8},{8,9},{9,10},{10,1... | collective-permute-start | bytes 1769480 | tf_op jit(solution)/shard_map/while/body/eval_jaxpr/ppermute | solution.py:14
  306.1 15.8 %collective-permute-start.3 = (f32[144,8,128]{2,0,1:T(8,128)}, f32[144,8,128]{2,0,1:T(8,128)}, u32[]{:S(2)}, u32[]{:S(2)}) collective-permute-start(f32[144,8,128]{2,0,1:T(8,128)} %fusion.63), channel_id=1, source_target_pairs={{0,1},{1,2},{2,3},{3,4},{4,5},{5,6},{6,7},{7,8},{8,9},{9,10},{10,1... | collective-permute-start | bytes 1769480 | tf_op jit(solution)/shard_map/while/body/eval_jaxpr/ppermute | solution.py:14
  325.4 25.6 %collective-permute-start.2 = (f32[144,8,128]{2,0,1:T(8,128)S(1)}, f32[144,8,128]{2,0,1:T(8,128)S(1)}, u32[]{:S(2)}, u32[]{:S(2)}) collective-permute-start(f32[144,8,128]{2,0,1:T(8,128)S(1)} %fusion.61), channel_id=1, source_target_pairs={{0,1},{1,2},{2,3},{3,4},{4,5},{5,6},{6,7},{7,8},{8,9},{9,10},{10,1... | collective-permute-start | bytes 1769480 | tf_op jit(solution)/shard_map/while/body/eval_jaxpr/ppermute | solution.py:14
  335.2 15.8 %collective-permute-start.3 = (f32[144,8,128]{2,0,1:T(8,128)}, f32[144,8,128]{2,0,1:T(8,128)}, u32[]{:S(2)}, u32[]{:S(2)}) collective-permute-start(f32[144,8,128]{2,0,1:T(8,128)} %fusion.63), channel_id=1, source_target_pairs={{0,1},{1,2},{2,3},{3,4},{4,5},{5,6},{6,7},{7,8},{8,9},{9,10},{10,1... | collective-permute-start | bytes 1769480 | tf_op jit(solution)/shard_map/while/body/eval_jaxpr/ppermute | solution.py:14
  354.5 25.6 %collective-permute-start.2 = (f32[144,8,128]{2,0,1:T(8,128)S(1)}, f32[144,8,128]{2,0,1:T(8,128)S(1)}, u32[]{:S(2)}, u32[]{:S(2)}) collective-permute-start(f32[144,8,128]{2,0,1:T(8,128)S(1)} %fusion.61), channel_id=1, source_target_pairs={{0,1},{1,2},{2,3},{3,4},{4,5},{5,6},{6,7},{7,8},{8,9},{9,10},{10,1... | collective-permute-start | bytes 1769480 | tf_op jit(solution)/shard_map/while/body/eval_jaxpr/ppermute | solution.py:14
  364.4 15.8 %collective-permute-start.3 = (f32[144,8,128]{2,0,1:T(8,128)}, f32[144,8,128]{2,0,1:T(8,128)}, u32[]{:S(2)}, u32[]{:S(2)}) collective-permute-start(f32[144,8,128]{2,0,1:T(8,128)} %fusion.63), channel_id=1, source_target_pairs={{0,1},{1,2},{2,3},{3,4},{4,5},{5,6},{6,7},{7,8},{8,9},{9,10},{10,1... | collective-permute-start | bytes 1769480 | tf_op jit(solution)/shard_map/while/body/eval_jaxpr/ppermute | solution.py:14
  383.7 25.6 %collective-permute-start.2 = (f32[144,8,128]{2,0,1:T(8,128)S(1)}, f32[144,8,128]{2,0,1:T(8,128)S(1)}, u32[]{:S(2)}, u32[]{:S(2)}) collective-permute-start(f32[144,8,128]{2,0,1:T(8,128)S(1)} %fusion.61), channel_id=1, source_target_pairs={{0,1},{1,2},{2,3},{3,4},{4,5},{5,6},{6,7},{7,8},{8,9},{9,10},{10,1... | collective-permute-start | bytes 1769480 | tf_op jit(solution)/shard_map/while/body/eval_jaxpr/ppermute | solution.py:14
  393.5 15.8 %collective-permute-start.3 = (f32[144,8,128]{2,0,1:T(8,128)}, f32[144,8,128]{2,0,1:T(8,128)}, u32[]{:S(2)}, u32[]{:S(2)}) collective-permute-start(f32[144,8,128]{2,0,1:T(8,128)} %fusion.63), channel_id=1, source_target_pairs={{0,1},{1,2},{2,3},{3,4},{4,5},{5,6},{6,7},{7,8},{8,9},{9,10},{10,1... | collective-permute-start | bytes 1769480 | tf_op jit(solution)/shard_map/while/body/eval_jaxpr/ppermute | solution.py:14
  412.8 25.6 %collective-permute-start.2 = (f32[144,8,128]{2,0,1:T(8,128)S(1)}, f32[144,8,128]{2,0,1:T(8,128)S(1)}, u32[]{:S(2)}, u32[]{:S(2)}) collective-permute-start(f32[144,8,128]{2,0,1:T(8,128)S(1)} %fusion.61), channel_id=1, source_target_pairs={{0,1},{1,2},{2,3},{3,4},{4,5},{5,6},{6,7},{7,8},{8,9},{9,10},{10,1... | collective-permute-start | bytes 1769480 | tf_op jit(solution)/shard_map/while/body/eval_jaxpr/ppermute | solution.py:14
  422.6 15.8 %collective-permute-start.3 = (f32[144,8,128]{2,0,1:T(8,128)}, f32[144,8,128]{2,0,1:T(8,128)}, u32[]{:S(2)}, u32[]{:S(2)}) collective-permute-start(f32[144,8,128]{2,0,1:T(8,128)} %fusion.63), channel_id=1, source_target_pairs={{0,1},{1,2},{2,3},{3,4},{4,5},{5,6},{6,7},{7,8},{8,9},{9,10},{10,1... | collective-permute-start | bytes 1769480 | tf_op jit(solution)/shard_map/while/body/eval_jaxpr/ppermute | solution.py:14
  441.9 25.6 %collective-permute-start.2 = (f32[144,8,128]{2,0,1:T(8,128)S(1)}, f32[144,8,128]{2,0,1:T(8,128)S(1)}, u32[]{:S(2)}, u32[]{:S(2)}) collective-permute-start(f32[144,8,128]{2,0,1:T(8,128)S(1)} %fusion.61), channel_id=1, source_target_pairs={{0,1},{1,2},{2,3},{3,4},{4,5},{5,6},{6,7},{7,8},{8,9},{9,10},{10,1... | collective-permute-start | bytes 1769480 | tf_op jit(solution)/shard_map/while/body/eval_jaxpr/ppermute | solution.py:14
  451.7 15.8 %collective-permute-start.3 = (f32[144,8,128]{2,0,1:T(8,128)}, f32[144,8,128]{2,0,1:T(8,128)}, u32[]{:S(2)}, u32[]{:S(2)}) collective-permute-start(f32[144,8,128]{2,0,1:T(8,128)} %fusion.63), channel_id=1, source_target_pairs={{0,1},{1,2},{2,3},{3,4},{4,5},{5,6},{6,7},{7,8},{8,9},{9,10},{10,1... | collective-permute-start | bytes 1769480 | tf_op jit(solution)/shard_map/while/body/eval_jaxpr/ppermute | solution.py:14
  471.0 25.6 %collective-permute-start.2 = (f32[144,8,128]{2,0,1:T(8,128)S(1)}, f32[144,8,128]{2,0,1:T(8,128)S(1)}, u32[]{:S(2)}, u32[]{:S(2)}) collective-permute-start(f32[144,8,128]{2,0,1:T(8,128)S(1)} %fusion.61), channel_id=1, source_target_pairs={{0,1},{1,2},{2,3},{3,4},{4,5},{5,6},{6,7},{7,8},{8,9},{9,10},{10,1... | collective-permute-start | bytes 1769480 | tf_op jit(solution)/shard_map/while/body/eval_jaxpr/ppermute | solution.py:14
  480.8 15.8 %collective-permute-start.3 = (f32[144,8,128]{2,0,1:T(8,128)}, f32[144,8,128]{2,0,1:T(8,128)}, u32[]{:S(2)}, u32[]{:S(2)}) collective-permute-start(f32[144,8,128]{2,0,1:T(8,128)} %fusion.63), channel_id=1, source_target_pairs={{0,1},{1,2},{2,3},{3,4},{4,5},{5,6},{6,7},{7,8},{8,9},{9,10},{10,1... | collective-permute-start | bytes 1769480 | tf_op jit(solution)/shard_map/while/body/eval_jaxpr/ppermute | solution.py:14
  500.1 25.6 %collective-permute-start.2 = (f32[144,8,128]{2,0,1:T(8,128)S(1)}, f32[144,8,128]{2,0,1:T(8,128)S(1)}, u32[]{:S(2)}, u32[]{:S(2)}) collective-permute-start(f32[144,8,128]{2,0,1:T(8,128)S(1)} %fusion.61), channel_id=1, source_target_pairs={{0,1},{1,2},{2,3},{3,4},{4,5},{5,6},{6,7},{7,8},{8,9},{9,10},{10,1... | collective-permute-start | bytes 1769480 | tf_op jit(solution)/shard_map/while/body/eval_jaxpr/ppermute | solution.py:14
  510.0 15.8 %collective-permute-start.3 = (f32[144,8,128]{2,0,1:T(8,128)}, f32[144,8,128]{2,0,1:T(8,128)}, u32[]{:S(2)}, u32[]{:S(2)}) collective-permute-start(f32[144,8,128]{2,0,1:T(8,128)} %fusion.63), channel_id=1, source_target_pairs={{0,1},{1,2},{2,3},{3,4},{4,5},{5,6},{6,7},{7,8},{8,9},{9,10},{10,1... | collective-permute-start | bytes 1769480 | tf_op jit(solution)/shard_map/while/body/eval_jaxpr/ppermute | solution.py:14
  529.3 25.6 %collective-permute-start.2 = (f32[144,8,128]{2,0,1:T(8,128)S(1)}, f32[144,8,128]{2,0,1:T(8,128)S(1)}, u32[]{:S(2)}, u32[]{:S(2)}) collective-permute-start(f32[144,8,128]{2,0,1:T(8,128)S(1)} %fusion.61), channel_id=1, source_target_pairs={{0,1},{1,2},{2,3},{3,4},{4,5},{5,6},{6,7},{7,8},{8,9},{9,10},{10,1... | collective-permute-start | bytes 1769480 | tf_op jit(solution)/shard_map/while/body/eval_jaxpr/ppermute | solution.py:14
  539.1 15.8 %collective-permute-start.3 = (f32[144,8,128]{2,0,1:T(8,128)}, f32[144,8,128]{2,0,1:T(8,128)}, u32[]{:S(2)}, u32[]{:S(2)}) collective-permute-start(f32[144,8,128]{2,0,1:T(8,128)} %fusion.63), channel_id=1, source_target_pairs={{0,1},{1,2},{2,3},{3,4},{4,5},{5,6},{6,7},{7,8},{8,9},{9,10},{10,1... | collective-permute-start | bytes 1769480 | tf_op jit(solution)/shard_map/while/body/eval_jaxpr/ppermute | solution.py:14
  558.4 25.6 %collective-permute-start.2 = (f32[144,8,128]{2,0,1:T(8,128)S(1)}, f32[144,8,128]{2,0,1:T(8,128)S(1)}, u32[]{:S(2)}, u32[]{:S(2)}) collective-permute-start(f32[144,8,128]{2,0,1:T(8,128)S(1)} %fusion.61), channel_id=1, source_target_pairs={{0,1},{1,2},{2,3},{3,4},{4,5},{5,6},{6,7},{7,8},{8,9},{9,10},{10,1... | collective-permute-start | bytes 1769480 | tf_op jit(solution)/shard_map/while/body/eval_jaxpr/ppermute | solution.py:14
  568.2 15.8 %collective-permute-start.3 = (f32[144,8,128]{2,0,1:T(8,128)}, f32[144,8,128]{2,0,1:T(8,128)}, u32[]{:S(2)}, u32[]{:S(2)}) collective-permute-start(f32[144,8,128]{2,0,1:T(8,128)} %fusion.63), channel_id=1, source_target_pairs={{0,1},{1,2},{2,3},{3,4},{4,5},{5,6},{6,7},{7,8},{8,9},{9,10},{10,1... | collective-permute-start | bytes 1769480 | tf_op jit(solution)/shard_map/while/body/eval_jaxpr/ppermute | solution.py:14
  585.1 16.1 %all-to-all-start.6 = ((bf16[16,9,1024]{2,1,0:T(8,128)(2,1)}), bf16[16,9,1024]{2,1,0:T(8,128)(2,1)S(1)}, u32[]{:S(2)}, u32[]{:S(2)}) async-start(bf16[16,9,1024]{2,1,0:T(8,128)(2,1)} %convert_element_type.113), calls=%async_computation.6 | async-start | bytes 1048576 | tf_op jit(solution)/shard_map/all_to_all | solution.py:129
  601.3 17.0 %all-to-all-start.7 = ((bf16[16,9,1024]{2,1,0:T(8,128)(2,1)}), bf16[16,9,1024]{2,1,0:T(8,128)(2,1)S(1)}, u32[]{:S(2)}, u32[]{:S(2)}) async-start(bf16[16,9,1024]{2,1,0:T(8,128)(2,1)} %convert_element_type.115), calls=%async_computation.7 | async-start | bytes 1048576 | tf_op jit(solution)/shard_map/all_to_all | solution.py:130
  638.9 22.7 %all-to-all-start.9 = ((bf16[16,9,1024]{2,1,0:T(8,128)(2,1)}), bf16[16,9,1024]{2,1,0:T(8,128)(2,1)S(1)}, u32[]{:S(2)}, u32[]{:S(2)}) async-start(bf16[16,9,1024]{2,1,0:T(8,128)(2,1)} %get-tuple-element.434), calls=%async_computation.9 | async-start | bytes 1048576 | tf_op jit(solution)/shard_map/all_to_all | solution.py:132
  (36 other events, 335.7 us)
where the time goes:
time: 665 us; the launch traced here: 663 us
  waiting for transfers between devices  267 us (40%)
  starting transfers between devices  242 us (36%)
  matrix products  86 us (13%)
  local copies, waits for them, and re-layouts  34.8 us (5%)
  blocking collectives  20.6 us (3%)
  other arithmetic  11.3 us (2%)
    ppermute x64, starting transfers between devices, from_behind(): lax.ppermute(array, axis, [(i, (i + by) % length) for i in range(length)])  191 us
    ppermute x64, waiting for transfers between devices, from_behind(): lax.ppermute(array, axis, [(i, (i + by) % length) for i in range(length)])  160 us
    dot_general x16, matrix products, attend(): jnp.einsum('hpr,phd->rhd', weight, do_heads, preferred_element_type=jnp.f...  41.5 us
    dot_general x16, matrix products, attend(): jnp.einsum('phd,rhd->hpr', do_heads, v_heads, preferred_element_type=jnp....  27.1 us
    all_to_all x1, blocking collectives, local(): lax.all_to_all(to_sources(dv_total), 'dp', split_axis=0, concat_axis=0, t...  20.6 us
    all_to_all x1, waiting for transfers between devices, local(): lax.all_to_all(to_buckets(attn_out), 'dp', split_axis=0, concat_axis=0, t...  14.2 us
    all_to_all x1, waiting for transfers between devices, local(): lax.all_to_all(to_buckets(values), 'dp', split_axis=0, concat_axis=0, til...  13.6 us
  transfers between devices with their start and end apart: 73, of which 41 were waited for; matrix products, arithmetic and copies ran while one was open for 10% of the time, Pallas kernels for 0%

commit v1 on v0

v1 whole, which is shorter than its diff:
```python
import math

import jax
import jax.numpy as jnp
from jax import lax
from jax.experimental import pallas as pl
from jax.experimental.pallas import tpu as pltpu
from jax.sharding import PartitionSpec as P

D = 1024
HEADS = 8
HD = 128
ROWS = 144
HALF = 72
PADH = 80
BLK = 9
NDP = 16
NZ = 8
NCTX = 16
NM = 8
USERS = 4
ATT_DIV = 32
RT = 160
PB = 256
NRT = 8
NPB = 10
MESH = pl.DeviceIdType.MESH
F32 = jnp.float32
BF16 = jnp.bfloat16
NT = (((1,), (1,)), ((), ()))


def p_blocks(rt):
    return (rt, NPB) if rt < 4 else (5, 7 + rt - 4)


def kernel(
    tgt, lens, q_ref, k_ref, v_ref, u_ref, o_ref, dy_ref,
    oq_ref, ok_ref, ov_ref, ou_ref,
    scr, sb_qk, rb_qk, sb_1, rb_1, sa, qd, kv, w_buf, f_buf, ds_buf,
    dq_buf, xs, xr, g2, r2, sb2, rb2,
    ss_b, rs_b, ss_a, rs_a, ss_f, rs_f, ss_x, rs_x, ss_a2, rs_a2, ss_b2, rs_b2,
):
    dp = lax.axis_index("dp")
    ctx = lax.axis_index("ctx")
    xlo, z = dp // NZ, dp % NZ
    m, kap = ctx // 2, ctx % 2
    scale = 1.0 / math.sqrt(HD)

    def dp_peer(d):
        return ((xlo + d) % 2) * NZ + (z + d // 2) % NZ

    def m_peer(e):
        return (m + e) % NM

    barrier = pltpu.get_barrier_semaphore()

    def greet_dp(d, c):
        pl.semaphore_signal(barrier, inc=1, device_id=(dp_peer(d), ctx), device_id_type=MESH)
        return c

    def greet_m(e, c):
        pl.semaphore_signal(barrier, inc=1, device_id=(dp, m_peer(e) * 2 + kap), device_id_type=MESH)
        return c

    lax.fori_loop(1, NDP, greet_dp, 0)
    lax.fori_loop(1, NM, greet_m, 0)
    pl.semaphore_signal(barrier, inc=1, device_id=(dp, m * 2 + 1 - kap), device_id_type=MESH)

    row = lax.broadcasted_iota(jnp.int32, (ROWS, ROWS), 0)
    col = lax.broadcasted_iota(jnp.int32, (ROWS, ROWS), 1)
    shift_c = jnp.zeros((ROWS, ROWS), jnp.int32)
    shift_r = jnp.zeros((ROWS, ROWS), jnp.int32)
    for b in range(NDP):
        by = (tgt[0, b] - b) * BLK
        shift_c = jnp.where((col >= b * BLK) & (col < b * BLK + BLK), by, shift_c)
        shift_r = jnp.where((row >= b * BLK) & (row < b * BLK + BLK), by, shift_r)
    to_stream = jnp.where(row == col + shift_c, 1.0, 0.0).astype(BF16)
    to_arrival = jnp.where(col == row + shift_r, 1.0, 0.0).astype(BF16)

    def pack_b(arrays, dst):
        n = len(arrays) * HEADS
        for a, x in enumerate(arrays):
            y = jnp.dot(to_stream, x, preferred_element_type=F32)
            for h in range(HEADS):
                scr[pl.ds(a * HEADS + h, ROWS, stride=n), :] = y[:, h * HD:(h + 1) * HD]
        size = dst.shape[1]
        for j in range(NDP):
            dst[j] = scr[j * BLK * n:j * BLK * n + size, :].astype(BF16)

    def copy_b(src, dst, ch, peer, ssem, rsem):
        return pltpu.make_async_remote_copy(
            src_ref=src.at[peer], dst_ref=dst.at[dp], send_sem=ssem.at[ch, peer], recv_sem=rsem.at[ch, dp],
            device_id=(peer, ctx), device_id_type=MESH)

    def arrival_b(src, dst, ch, peer, ssem, rsem):
        return pltpu.make_async_remote_copy(
            src_ref=src.at[peer], dst_ref=dst.at[peer], send_sem=ssem.at[ch, peer], recv_sem=rsem.at[ch, peer],
            device_id=(peer, ctx), device_id_type=MESH)

    def send_b(src, dst, ch, ssem, rsem):
        def step(d, c):
            copy_b(src, dst, ch, dp_peer(d), ssem, rsem).start()
            return c

        lax.fori_loop(1, NDP, step, 0)
        dst[dp] = src[dp]

    def wait_b(src, dst, ch, ssem, rsem):
        def step(d, c):
            arrival_b(src, dst, ch, dp_peer(d), ssem, rsem).wait_recv()
            return c

        lax.fori_loop(1, NDP, step, 0)

    def drain_b(src, dst, ch, ssem, rsem):
        def step(d, c):
            copy_b(src, dst, ch, dp_peer(d), ssem, rsem).wait_send()
            return c

        lax.fori_loop(1, NDP, step, 0)

    zeros8 = jnp.zeros((PADH - HALF, HD), F32)

    def pack_a(src, arrays):
        n = len(arrays) * HEADS
        for i in range(NDP):
            scr[i * BLK * n:(i + 1) * BLK * n, :] = src[i][:BLK * n].astype(F32)
        for a, arr in enumerate(arrays):
            for h in range(HEADS):
                x = scr[pl.ds(a * HEADS + h, ROWS, stride=n), :]
                sa[arr, h, 0] = jnp.concatenate([x[:HALF], zeros8], axis=0).astype(BF16)
                sa[arr, h, 1] = jnp.concatenate([x[HALF:], zeros8], axis=0).astype(BF16)

    def slot_a(arr, mm):
        return qd.at[arr // 2, :, mm * 2 + kap] if arr % 2 == 0 else kv.at[arr // 2, :, mm]

    def copy_a(arr, peer):
        return pltpu.make_async_remote_copy(
            src_ref=sa.at[arr, peer], dst_ref=slot_a(arr, m), send_sem=ss_a.at[arr, peer], recv_sem=rs_a.at[arr, m],
            device_id=(dp, peer * 2 + kap), device_id_type=MESH)

    def arrival_a(arr, peer):
        return pltpu.make_async_remote_copy(
            src_ref=sa.at[arr, peer], dst_ref=slot_a(arr, peer), send_sem=ss_a.at[arr, peer], recv_sem=rs_a.at[arr, peer],
            device_id=(dp, peer * 2 + kap), device_id_type=MESH)

    def send_a(arr):
        def step(e, c):
            copy_a(arr, m_peer(e)).start()
            return c

        lax.fori_loop(1, NM, step, 0)
        if arr % 2 == 0:
            qd[arr // 2, :, ctx] = sa[arr, m]
        else:
            kv[arr // 2, :, m] = sa[arr, m]

    def copy_f(a, mm, par):
        ref = qd.at[a, :, mm * 2 + par]
        return pltpu.make_async_remote_copy(
            src_ref=ref, dst_ref=ref, send_sem=ss_f.at[a, mm], recv_sem=rs_f.at[a, mm],
            device_id=(dp, m * 2 + 1 - kap), device_id_type=MESH)

    def wait_a(arr):
        def step(e, c):
            arrival_a(arr, m_peer(e)).wait_recv()
            if arr % 2 == 0:
                copy_f(arr // 2, m_peer(e), kap).start()
            return c

        if arr % 2 == 0:
            copy_f(arr // 2, m, kap).start()
        lax.fori_loop(1, NM, step, 0)

    def wait_f(a):
        def step(e, c):
            copy_f(a, m_peer(e), 1 - kap).wait_recv()
            return c

        lax.fori_loop(0, NM, step, 0)

    pack_b([q_ref[...], k_ref[...]], sb_qk)
    pl.semaphore_wait(barrier, NDP - 1 + NM - 1 + 1)
    send_b(sb_qk, rb_qk, 0, ss_b, rs_b)

    o_full = o_ref[...].astype(F32)
    centred = o_full - jnp.mean(o_full, axis=1, keepdims=True)
    inv_std = 1.0 / jnp.sqrt(jnp.mean(centred * centred, axis=1, keepdims=True) + 1e-05)
    normed = centred * inv_std
    dy_full = dy_ref[...].astype(F32)
    ou_ref[...] = (dy_full * normed).astype(BF16)
    g_term = dy_full * u_ref[...].astype(F32)
    d_o = inv_std * (
        g_term
        - jnp.mean(g_term, axis=1, keepdims=True)
        - normed * jnp.mean(g_term * normed, axis=1, keepdims=True)
    )
    pack_b([d_o.astype(BF16)], sb_1.at[0])
    send_b(sb_1.at[0], rb_1.at[0], 1, ss_b, rs_b)
    pack_b([v_ref[...]], sb_1.at[1])
    send_b(sb_1.at[1], rb_1.at[1], 2, ss_b, rs_b)

    wait_b(sb_qk, rb_qk, 0, ss_b, rs_b)
    pack_a(rb_qk, [0, 1])
    send_a(0)
    send_a(1)

    lane = lax.broadcasted_iota(jnp.int32, (8, PB), 1)
    sub = lax.broadcasted_iota(jnp.int32, (RT, PB), 0)
    ends = []
    total = jnp.int32(0)
    for user in range(USERS):
        total = total + lens[0, user]
        ends.append(total)

    def query_places(b):
        lane_at = lane + b * PB
        late = lane_at >= NCTX * PADH
        lane_in = lane_at - jnp.where(late, NCTX * PADH, 0)
        chunk = jnp.zeros_like(lane_in)
        for c in range(1, NCTX):
            chunk = chunk + jnp.where(lane_in >= c * PADH, 1, 0)
        inner = lane_in - chunk * PADH
        place = jnp.where(late, 2 * NCTX - 1 - chunk, chunk) * HALF + inner
        first = jnp.zeros_like(place)
        for user in range(USERS - 1):
            first = jnp.maximum(first, jnp.where(ends[user] <= place, ends[user], 0))
        return place[:1], first[:1]

    def key_places(rt):
        t = rt % 4
        second = sub >= PADH
        c = 2 * (2 * t + jnp.where(second, 1, 0)) + kap
        chunk = c if rt < 4 else 2 * NCTX - 1 - c
        return chunk * HALF + sub - jnp.where(second, PADH, 0)

    def q_at(a, b):
        return qd.at[a].reshape(2 * NCTX * PADH, HD)[pl.ds(pl.multiple_of(b * PB, PB), PB), :]

    def k_at(a, rt):
        return kv.at[a].reshape(2 * NM * PADH, HD)[rt * RT:(rt + 1) * RT, :]

    wait_a(0)
    wait_a(1)
    wait_f(0)

    for rt in range(NRT):
        keys = k_at(0, rt)
        key_place = key_places(rt)

        def score_step(b, c, rt=rt, keys=keys, key_place=key_place):
            place, first = query_places(b)
            s = lax.dot_general(keys, q_at(0, b), NT, preferred_element_type=F32) * scale
            sig = 0.5 * jnp.tanh(0.5 * s) + 0.5
            sig = jnp.where((key_place <= place) & (key_place >= first), sig, 0.0)
            w = s * sig
            w_buf[rt, b] = w.astype(BF16)
            f_buf[rt, b] = sig * (1.0 - w) + w
            return c

        lax.fori_loop(*p_blocks(rt), score_step, 0)

    wait_b(sb_1.at[0], rb_1.at[0], 1, ss_b, rs_b)
    pack_a(rb_1.at[0], [2])
    send_a(2)
    wait_a(2)
    wait_f(1)

    def copy_a2(g, peer):
        return pltpu.make_async_remote_copy(
            src_ref=g2.at[g, peer], dst_ref=r2.at[g, m], send_sem=ss_a2.at[g, peer], recv_sem=rs_a2.at[g, m],
            device_id=(dp, peer * 2 + kap), device_id_type=MESH)

    def arrival_a2(g, peer):
        return pltpu.make_async_remote_copy(
            src_ref=g2.at[g, peer], dst_ref=r2.at[g, peer], send_sem=ss_a2.at[g, peer], recv_sem=rs_a2.at[g, peer],
            device_id=(dp, peer * 2 + kap), device_id_type=MESH)

    def send_a2(g):
        def step(e, c):
            copy_a2(g, m_peer(e)).start()
            return c

        lax.fori_loop(1, NM, step, 0)
        r2[g, m] = g2[g, m]

    def send_b2(g):
        def step(e, c):
            arrival_a2(g, m_peer(e)).wait_recv()
            return c

        lax.fori_loop(1, NM, step, 0)
        for h in range(HEADS):
            scr[pl.ds(h, HALF, stride=HEADS), :] = r2[g, h, 0].astype(F32)[:HALF]
            scr[pl.ds(HALF * HEADS + h, HALF, stride=HEADS), :] = r2[g, h, 1].astype(F32)[:HALF]
        for i in range(NDP):
            sb2[g, i] = scr[i * HALF:i * HALF + PADH, :].astype(BF16)
        send_b(sb2.at[g], rb2.at[g], g, ss_b2, rs_b2)

    def put_keys_grad(g, rt, value):
        t, half = rt % 4, rt // 4
        g2[g, 2 * t, half] = value[:PADH].astype(BF16)
        g2[g, 2 * t + 1, half] = value[PADH:].astype(BF16)

    for rt in range(NRT):
        def dv_step(b, acc, rt=rt):
            return acc + jnp.dot(w_buf[rt, b], q_at(1, b), preferred_element_type=F32)

        acc = lax.fori_loop(*p_blocks(rt), dv_step, jnp.zeros((RT, HD), F32))
        put_keys_grad(0, rt, acc * (1.0 / ATT_DIV))
    send_a2(0)

    wait_b(sb_1.at[1], rb_1.at[1], 2, ss_b, rs_b)
    pack_a(rb_1.at[1], [3])
    send_a(3)
    send_b2(0)
    wait_a(3)

    for rt in range(NRT):
        values = k_at(1, rt)

        def dk_step(b, acc, rt=rt, values=values):
            dw = lax.dot_general(values, q_at(1, b), NT, preferred_element_type=F32)
            ds = (dw * f_buf[rt, b]).astype(BF16)
            ds_buf[rt, b] = ds
            return acc + jnp.dot(ds, q_at(0, b), preferred_element_type=F32)

        acc = lax.fori_loop(*p_blocks(rt), dk_step, jnp.zeros((RT, HD), F32))
        put_keys_grad(1, rt, acc * (scale / ATT_DIV))
    send_a2(1)

    for b in range(NPB):
        acc = jnp.zeros((HD, PB), F32)
        for rt in range(NRT):
            lo, hi = p_blocks(rt)
            if lo <= b < hi:
                acc = acc + jnp.dot(k_at(0, rt).T, ds_buf[rt, b], preferred_element_type=F32)
        dq_buf[b * PB:(b + 1) * PB, :] = acc.T * (scale / ATT_DIV)

    dq_view = dq_buf.reshape(2, NM, 2, PADH, HD)
    xs[...] = dq_view[:, :, 1 - kap]
    swap = pltpu.make_async_remote_copy(
        src_ref=xs, dst_ref=xr, send_sem=ss_x, recv_sem=rs_x,
        device_id=(dp, m * 2 + 1 - kap), device_id_type=MESH)
    swap.start()
    send_b2(1)
    swap.wait_recv()
    for mm in range(NM):
        g2[2, mm] = (dq_view[:, mm, kap] + xr[:, mm]).astype(BF16)
    send_a2(2)
    send_b2(2)

    for g, out in ((0, ov_ref), (1, ok_ref), (2, oq_ref)):
        wait_b(sb2.at[g], rb2.at[g], g, ss_b2, rs_b2)
        for j in range(NDP):
            scr[j * HALF:(j + 1) * HALF, :] = rb2[g, j][:HALF].astype(F32)
        rows = jnp.concatenate(
            [scr[pl.ds(h, ROWS, stride=HEADS), :].astype(BF16) for h in range(HEADS)], axis=1)
        out[...] = jnp.dot(to_arrival, rows, preferred_element_type=F32).astype(BF16)

    drain_b(sb_qk, rb_qk, 0, ss_b, rs_b)
    drain_b(sb_1.at[0], rb_1.at[0], 1, ss_b, rs_b)
    drain_b(sb_1.at[1], rb_1.at[1], 2, ss_b, rs_b)
    for g in range(3):
        drain_b(sb2.at[g], rb2.at[g], g, ss_b2, rs_b2)

    def drain_m(e, c):
        for arr in range(4):
            copy_a(arr, m_peer(e)).wait_send()
        for g in range(3):
            copy_a2(g, m_peer(e)).wait_send()
        return c

    lax.fori_loop(1, NM, drain_m, 0)

    def drain_f(e, c):
        for a in range(2):
            copy_f(a, e, kap).wait_send()
        return c

    lax.fori_loop(0, NM, drain_f, 0)
    swap.wait_send()


def local(queries, keys, values, gates, attn_out, grad_out, route, lengths):
    vmem = pl.BlockSpec(memory_space=pltpu.VMEM)
    smem = pl.BlockSpec(memory_space=pltpu.SMEM)
    dma = pltpu.SemaphoreType.DMA
    shape = jax.ShapeDtypeStruct((ROWS, D), BF16)
    outs = pl.pallas_call(
        kernel,
        name="hstu_backward",
        out_shape=[shape] * 4,
        in_specs=[smem] * 2 + [vmem] * 6,
        out_specs=[vmem] * 4,
        scratch_shapes=[
            pltpu.VMEM((ROWS * 16, HD), F32),
            pltpu.VMEM((NDP, ROWS, HD), BF16),
            pltpu.VMEM((NDP, ROWS, HD), BF16),
            pltpu.VMEM((2, NDP, PADH, HD), BF16),
            pltpu.VMEM((2, NDP, PADH, HD), BF16),
            pltpu.VMEM((4, NM, 2, PADH, HD), BF16),
            pltpu.VMEM((2, 2, NCTX, PADH, HD), BF16),
            pltpu.VMEM((2, 2, NM, PADH, HD), BF16),
            pltpu.VMEM((NRT, NPB, RT, PB), BF16),
            pltpu.VMEM((NRT, NPB, RT, PB), F32),
            pltpu.VMEM((NRT, NPB, RT, PB), BF16),
            pltpu.VMEM((NPB * PB, HD), F32),
            pltpu.VMEM((2, NM, PADH, HD), F32),
            pltpu.VMEM((2, NM, PADH, HD), F32),
            pltpu.VMEM((3, NM, 2, PADH, HD), BF16),
            pltpu.VMEM((3, NM, 2, PADH, HD), BF16),
            pltpu.VMEM((3, NDP, PADH, HD), BF16),
            pltpu.VMEM((3, NDP, PADH, HD), BF16),
            dma((3, NDP)), dma((3, NDP)),
            dma((4, NM)), dma((4, NM)),
            dma((2, NM)), dma((2, NM)),
            dma, dma,
            dma((3, NM)), dma((3, NM)),
            dma((3, NDP)), dma((3, NDP)),
        ],
        compiler_params=pltpu.CompilerParams(
            collective_id=0, has_side_effects=True, vmem_limit_bytes=56 * 1024 * 1024
        ),
        cost_estimate=pl.CostEstimate(flops=3_400_000_000, bytes_accessed=3_000_000, transcendentals=2_000_000),
    )(route, lengths, queries[0], keys[0], values[0], gates[0], attn_out[0], grad_out[0])
    return tuple(x[None] for x in outs)


def solution(mesh):
    rows = P("dp", "ctx", None)
    return jax.shard_map(
        local,
        mesh=mesh,
        in_specs=(rows,) * 6 + (P("dp", "ctx"), P("dp", None)),
        out_specs=(rows,) * 4,
        check_vma=False,
    )
```

time: 665 us -> 132 us (0.20)
  waiting for transfers between devices: 267 us -> 0 us
  starting transfers between devices: 242 us -> 0 us
  Pallas kernels: 0 us -> 126 us
  matrix products: 86 us -> 0 us
  local copies, waits for them, and re-layouts: 34.8 us -> 4.59 us
  blocking collectives: 20.6 us -> 0 us
  other arithmetic: 11.3 us -> 0 us
    ppermute x64 -> x0, starting transfers between devices: 191 us -> none  [from_behind(): lax.ppermute(array, axis, [(i, (i + by) % length) for i in range(length)])]
    ppermute x64 -> x0, waiting for transfers between devices: 160 us -> none  [from_behind(): lax.ppermute(array, axis, [(i, (i + by) % length) for i in range(length)])]
    pallas_call x0 -> x1, Pallas kernels: none -> 126 us  [local(): pl.pallas_call(kernel, name='hstu_backward', out_shape=[shape] * 4, in_sp...]
    all_to_all x9 -> x0, waiting for transfers between devices: 106 us -> none  [the longest x1 14.2 us: local(): lax.all_to_all(to_buckets(attn_out), 'dp', split_axis=0, concat_axis=0, t...]
    dot_general x80 -> x0, matrix products: 86 us -> none  [the longest x16 41.5 us: attend(): jnp.einsum('hpr,phd->rhd', weight, do_heads, preferred_element_type=jnp.f...]
    all_to_all x9 -> x0, starting transfers between devices: 50.6 us -> none  [the longest x1 9.5 us: local(): lax.all_to_all(to_buckets(attn_out), 'dp', split_axis=0, concat_axis=0, t...]
    all_to_all x1 -> x0, blocking collectives: 20.6 us -> none  [local(): lax.all_to_all(to_sources(dv_total), 'dp', split_axis=0, concat_axis=0, t...]
    while x32 -> x0, local copies, waits for them, and re-layouts: 11.8 us -> none
  transfers between devices with their start and end apart: 73 -> 0, of which waited for: 41 -> 0; matrix products, arithmetic and copies ran while one was open for 10% -> 0% of each run, Pallas kernels for 0% -> 0%
where the time goes in v1:
time: 132 us
  Pallas kernels  126 us (95%)
  local copies, waits for them, and re-layouts  4.59 us (3%)
    pallas_call x1, Pallas kernels, local(): pl.pallas_call(kernel, name='hstu_backward', out_shape=[shape] * 4, in_sp...  126 us
    unnamed x10, local copies, waits for them, and re-layouts  4.59 us

profile of v1, /device:TPU:24, one launch (start us, length us, event | category | flops | bytes accessed | tf_op | source)
XLA Modules:
  0.0 131.7 jit_solution(4003249491694006357)
XLA Ops:
  0.6 126.4 %hstu_backward.1 = (bf16[144,1024]{1,0:T(8,128)(2,1)}, bf16[144,1024]{1,0:T(8,128)(2,1)}, bf16[144,1024]{1,0:T(8,128)(2,1)}, bf16[144,1024]{1,0:T(8,128)(2,1)}) custom-call(s32[1,16]{1,0:T(1,128)} %tgt.1, s32[1,4]{1,0:T(1,128)} %lens.1, bf16[144,1024]{1,0:T(8,128)(2,1)} %bitcast.14, bf16[144,1024]{1,0:T(8,128)(2,1)} %bitcast.15, bf16[144,1024]{1,0:T(8,128)(2,1)} %bitcast.16, ...), custom_call_target="tpu_custom_call" | custom-call | flops 3400000000 | bytes 3000000 | tf_op jit(solution)/shard_map/hstu_backward/pallas_call | solution.py:391
  127.1 0.0 copy-start.2
  127.1 1.7 %copy.16 = bf16[1,144,1024]{2,1,0:T(8,128)(2,1)} copy(bf16[1,144,1024]{2,1,0:T(8,128)(2,1)} %bitcast.13) | data formatting | bytes 589824
  128.8 0.0 copy-done.2
  128.8 0.0 copy-start.1
  128.8 0.7 copy.17
  129.5 0.4 copy-done.1
  129.9 0.0 copy-start
  129.9 0.7 copy.18
  130.6 0.4 copy-done
  131.0 0.7 copy.19
Async XLA Ops:
  127.1 1.8 %copy-start.2 = (bf16[144,1024]{1,0:T(8,128)(2,1)S(1)}, bf16[144,1024]{1,0:T(8,128)(2,1)}, u32[]{:S(2)}) copy-start(bf16[144,1024]{1,0:T(8,128)(2,1)} %get-tuple-element.9) | copy-start | bytes 884740
  128.8 1.1 copy-start.1
  129.9 1.1 copy-start

commit v2 on v1

--- a/solution.py
+++ b/solution.py
@@ -37,9 +37,9 @@
 def kernel(
     tgt, lens, q_ref, k_ref, v_ref, u_ref, o_ref, dy_ref,
     oq_ref, ok_ref, ov_ref, ou_ref,
-    scr, sb_qk, rb_qk, sb_1, rb_1, sa, qd, kv, w_buf, f_buf, ds_buf,
-    dq_buf, xs, xr, g2, r2, sb2, rb2,
-    ss_b, rs_b, ss_a, rs_a, ss_f, rs_f, ss_x, rs_x, ss_a2, rs_a2, ss_b2, rs_b2,
+    held, done, scr, sb_qk, rb_qk, sb_1, rb_1, sa, qd, kv, w_buf, f_buf, ds_buf,
+    dq_buf, xs, xr, g2, r2, sb2, rb2, at_query,
+    in_sem, out_sem, ss_b, rs_b, ss_a, rs_a, ss_f, rs_f, ss_x, rs_x, ss_a2, rs_a2, ss_b2, rs_b2,
 ):
     dp = lax.axis_index("dp")
     ctx = lax.axis_index("ctx")
@@ -52,6 +52,13 @@
 
     def m_peer(e):
         return (m + e) % NM
+
+    loads = [
+        pltpu.make_async_copy(ref, held.at[n], in_sem.at[n])
+        for n, ref in enumerate((q_ref, k_ref, o_ref, dy_ref, u_ref, v_ref))
+    ]
+    for load in loads:
+        load.start()
 
     barrier = pltpu.get_barrier_semaphore()
 
@@ -78,6 +85,8 @@
     to_stream = jnp.where(row == col + shift_c, 1.0, 0.0).astype(BF16)
     to_arrival = jnp.where(col == row + shift_r, 1.0, 0.0).astype(BF16)
 
+    drains = []
+
     def pack_b(arrays, dst):
         n = len(arrays) * HEADS
         for a, x in enumerate(arrays):
@@ -105,6 +114,7 @@
 
         lax.fori_loop(1, NDP, step, 0)
         dst[dp] = src[dp]
+        drains.append(lambda: drain_b(src, dst, ch, ssem, rsem))
 
     def wait_b(src, dst, ch, ssem, rsem):
         def step(d, c):
@@ -155,6 +165,14 @@
             qd[arr // 2, :, ctx] = sa[arr, m]
         else:
             kv[arr // 2, :, m] = sa[arr, m]
+        drains.append(lambda: drain_m(copy_a, arr))
+
+    def drain_m(copy, n):
+        def step(e, c):
+            copy(n, m_peer(e)).wait_send()
+            return c
+
+        lax.fori_loop(1, NM, step, 0)
 
     def copy_f(a, mm, par):
         ref = qd.at[a, :, mm * 2 + par]
@@ -171,8 +189,16 @@
 
         if arr % 2 == 0:
             copy_f(arr // 2, m, kap).start()
+            drains.append(lambda: drain_f(arr // 2))
         lax.fori_loop(1, NM, step, 0)
 
+    def drain_f(a):
+        def step(e, c):
+            copy_f(a, e, kap).wait_send()
+            return c
+
+        lax.fori_loop(0, NM, step, 0)
+
     def wait_f(a):
         def step(e, c):
             copy_f(a, m_peer(e), 1 - kap).wait_recv()
@@ -180,17 +206,24 @@
 
         lax.fori_loop(0, NM, step, 0)
 
-    pack_b([q_ref[...], k_ref[...]], sb_qk)
+    loads[0].wait()
+    loads[1].wait()
+    pack_b([held[0], held[1]], sb_qk)
     pl.semaphore_wait(barrier, NDP - 1 + NM - 1 + 1)
     send_b(sb_qk, rb_qk, 0, ss_b, rs_b)
 
-    o_full = o_ref[...].astype(F32)
+    for load in loads[2:5]:
+        load.wait()
+    o_full = held[2].astype(F32)
     centred = o_full - jnp.mean(o_full, axis=1, keepdims=True)
     inv_std = 1.0 / jnp.sqrt(jnp.mean(centred * centred, axis=1, keepdims=True) + 1e-05)
     normed = centred * inv_std
-    dy_full = dy_ref[...].astype(F32)
-    ou_ref[...] = (dy_full * normed).astype(BF16)
-    g_term = dy_full * u_ref[...].astype(F32)
+    dy_full = held[3].astype(F32)
+    done[3] = (dy_full * normed).astype(BF16)
+    store_u = pltpu.make_async_copy(done.at[3], ou_ref, out_sem.at[3])
+    store_u.start()
+    drains.append(store_u.wait)
+    g_term = dy_full * held[4].astype(F32)
     d_o = inv_std * (
         g_term
         - jnp.mean(g_term, axis=1, keepdims=True)
@@ -198,48 +231,49 @@
     )
     pack_b([d_o.astype(BF16)], sb_1.at[0])
     send_b(sb_1.at[0], rb_1.at[0], 1, ss_b, rs_b)
-    pack_b([v_ref[...]], sb_1.at[1])
+    loads[5].wait()
+    pack_b([held[5]], sb_1.at[1])
     send_b(sb_1.at[1], rb_1.at[1], 2, ss_b, rs_b)
 
-    wait_b(sb_qk, rb_qk, 0, ss_b, rs_b)
-    pack_a(rb_qk, [0, 1])
-    send_a(0)
-    send_a(1)
-
-    lane = lax.broadcasted_iota(jnp.int32, (8, PB), 1)
-    sub = lax.broadcasted_iota(jnp.int32, (RT, PB), 0)
     ends = []
     total = jnp.int32(0)
     for user in range(USERS):
         total = total + lens[0, user]
         ends.append(total)
-
-    def query_places(b):
-        lane_at = lane + b * PB
-        late = lane_at >= NCTX * PADH
-        lane_in = lane_at - jnp.where(late, NCTX * PADH, 0)
-        chunk = jnp.zeros_like(lane_in)
-        for c in range(1, NCTX):
-            chunk = chunk + jnp.where(lane_in >= c * PADH, 1, 0)
-        inner = lane_in - chunk * PADH
-        place = jnp.where(late, 2 * NCTX - 1 - chunk, chunk) * HALF + inner
-        first = jnp.zeros_like(place)
-        for user in range(USERS - 1):
-            first = jnp.maximum(first, jnp.where(ends[user] <= place, ends[user], 0))
-        return place[:1], first[:1]
+    lane = lax.broadcasted_iota(jnp.int32, (8, NPB * PB), 1)
+    late = lane >= NCTX * PADH
+    lane_in = lane - jnp.where(late, NCTX * PADH, 0)
+    chunk = jnp.zeros_like(lane_in)
+    for c in range(1, NCTX):
+        chunk = chunk + jnp.where(lane_in >= c * PADH, 1, 0)
+    place = jnp.where(late, 2 * NCTX - 1 - chunk, chunk) * HALF + lane_in - chunk * PADH
+    first = jnp.zeros_like(place)
+    for user in range(USERS - 1):
+        first = jnp.maximum(first, jnp.where(ends[user] <= place, ends[user], 0))
+    at_query[0] = place
+    at_query[1] = first
+
+    sub = lax.broadcasted_iota(jnp.int32, (RT, PB), 0)
+    second = jnp.where(sub >= PADH, 1, 0)
 
     def key_places(rt):
-        t = rt % 4
-        second = sub >= PADH
-        c = 2 * (2 * t + jnp.where(second, 1, 0)) + kap
-        chunk = c if rt < 4 else 2 * NCTX - 1 - c
-        return chunk * HALF + sub - jnp.where(second, PADH, 0)
-
-    def q_at(a, b):
-        return qd.at[a].reshape(2 * NCTX * PADH, HD)[pl.ds(pl.multiple_of(b * PB, PB), PB), :]
+        c = 2 * (2 * (rt % 4) + second) + kap
+        return (c if rt < 4 else 2 * NCTX - 1 - c) * HALF + sub - second * PADH
+
+    def q_at(a, lo, hi):
+        return qd.at[a].reshape(2 * NCTX * PADH, HD)[lo * PB:hi * PB, :]
 
     def k_at(a, rt):
         return kv.at[a].reshape(2 * NM * PADH, HD)[rt * RT:(rt + 1) * RT, :]
+
+    wait_b(sb_qk, rb_qk, 0, ss_b, rs_b)
+    pack_a(rb_qk, [0, 1])
+    send_a(0)
+    send_a(1)
+
+    wait_b(sb_1.at[0], rb_1.at[0], 1, ss_b, rs_b)
+    pack_a(rb_1.at[0], [2])
+    send_a(2)
 
     wait_a(0)
     wait_a(1)
@@ -249,21 +283,20 @@
         keys = k_at(0, rt)
         key_place = key_places(rt)
 
-        def score_step(b, c, rt=rt, keys=keys, key_place=key_place):
-            place, first = query_places(b)
-            s = lax.dot_general(keys, q_at(0, b), NT, preferred_element_type=F32) * scale
+        for b in range(*p_blocks(rt)):
+            at = slice(b * PB, (b + 1) * PB)
+            s = lax.dot_general(keys, q_at(0, b, b + 1), NT, preferred_element_type=F32) * scale
             sig = 0.5 * jnp.tanh(0.5 * s) + 0.5
-            sig = jnp.where((key_place <= place) & (key_place >= first), sig, 0.0)
+            live = (key_place <= at_query[0, :1, at]) & (key_place >= at_query[1, :1, at])
+            sig = jnp.where(live, sig, 0.0)
             w = s * sig
-            w_buf[rt, b] = w.astype(BF16)
-            f_buf[rt, b] = sig * (1.0 - w) + w
-            return c
-
-        lax.fori_loop(*p_blocks(rt), score_step, 0)
-
-    wait_b(sb_1.at[0], rb_1.at[0], 1, ss_b, rs_b)
-    pack_a(rb_1.at[0], [2])
-    send_a(2)
+            w_buf[rt, :, at] = w.astype(BF16)
+            f_buf[rt, :, at] = sig * (1.0 - w) + w
+
+    wait_b(sb_1.at[1], rb_1.at[1], 2, ss_b, rs_b)
+    pack_a(rb_1.at[1], [3])
+    send_a(3)
+
     wait_a(2)
     wait_f(1)
 
@@ -284,6 +317,7 @@
 
         lax.fori_loop(1, NM, step, 0)
         r2[g, m] = g2[g, m]
+        drains.append(lambda: drain_m(copy_a2, g))
 
     def send_b2(g):
         def step(e, c):
@@ -304,87 +338,70 @@
         g2[g, 2 * t + 1, half] = value[PADH:].astype(BF16)
 
     for rt in range(NRT):
-        def dv_step(b, acc, rt=rt):
-            return acc + jnp.dot(w_buf[rt, b], q_at(1, b), preferred_element_type=F32)
-
-        acc = lax.fori_loop(*p_blocks(rt), dv_step, jnp.zeros((RT, HD), F32))
+        lo, hi = p_blocks(rt)
+        acc = jnp.dot(w_buf[rt, :, lo * PB:hi * PB], q_at(1, lo, hi), preferred_element_type=F32)
         put_keys_grad(0, rt, acc * (1.0 / ATT_DIV))
     send_a2(0)
 
-    wait_b(sb_1.at[1], rb_1.at[1], 2, ss_b, rs_b)
-    pack_a(rb_1.at[1], [3])
-    send_a(3)
-    send_b2(0)
     wait_a(3)
 
     for rt in range(NRT):
         values = k_at(1, rt)
 
-        def dk_step(b, acc, rt=rt, values=values):
-            dw = lax.dot_general(values, q_at(1, b), NT, preferred_element_type=F32)
-            ds = (dw * f_buf[rt, b]).astype(BF16)
-            ds_buf[rt, b] = ds
-            return acc + jnp.dot(ds, q_at(0, b), preferred_element_type=F32)
-
-        acc = lax.fori_loop(*p_blocks(rt), dk_step, jnp.zeros((RT, HD), F32))
+        lo, hi = p_blocks(rt)
+        for b in range(lo, hi):
+            at = slice(b * PB, (b + 1) * PB)
+            dw = lax.dot_general(values, q_at(1, b, b + 1), NT, preferred_element_type=F32)
+            ds_buf[rt, :, at] = (dw * f_buf[rt, :, at]).astype(BF16)
+        acc = jnp.dot(ds_buf[rt, :, lo * PB:hi * PB], q_at(0, lo, hi), preferred_element_type=F32)
         put_keys_grad(1, rt, acc * (scale / ATT_DIV))
     send_a2(1)
-
-    for b in range(NPB):
-        acc = jnp.zeros((HD, PB), F32)
-        for rt in range(NRT):
-            lo, hi = p_blocks(rt)
-            if lo <= b < hi:
-                acc = acc + jnp.dot(k_at(0, rt).T, ds_buf[rt, b], preferred_element_type=F32)
-        dq_buf[b * PB:(b + 1) * PB, :] = acc.T * (scale / ATT_DIV)
+    send_b2(0)
 
     dq_view = dq_buf.reshape(2, NM, 2, PADH, HD)
-    xs[...] = dq_view[:, :, 1 - kap]
-    swap = pltpu.make_async_remote_copy(
-        src_ref=xs, dst_ref=xr, send_sem=ss_x, recv_sem=rs_x,
-        device_id=(dp, m * 2 + 1 - kap), device_id_type=MESH)
-    swap.start()
+
+    def swap(half):
+        return pltpu.make_async_remote_copy(
+            src_ref=xs.at[half], dst_ref=xr.at[half], send_sem=ss_x.at[half], recv_sem=rs_x.at[half],
+            device_id=(dp, m * 2 + 1 - kap), device_id_type=MESH)
+
+    for half in range(2):
+        for b in range(half * NPB // 2, (half + 1) * NPB // 2):
+            acc = jnp.zeros((HD, PB), F32)
+            for rt in range(NRT):
+                lo, hi = p_blocks(rt)
+                if lo <= b < hi:
+                    acc = acc + jnp.dot(
+                        k_at(0, rt).T, ds_buf[rt, :, b * PB:(b + 1) * PB], preferred_element_type=F32)
+            dq_buf[b * PB:(b + 1) * PB, :] = acc.T * (scale / ATT_DIV)
+        xs[half] = dq_view[half, :, 1 - kap]
+        swap(half).start()
+        drains.append(swap(half).wait_send)
+    for half in range(2):
+        swap(half).wait_recv()
+        for mm in range(NM):
+            g2[2, mm, half] = (dq_view[half, mm, kap] + xr[half, mm]).astype(BF16)
+    send_a2(2)
     send_b2(1)
-    swap.wait_recv()
-    for mm in range(NM):
-        g2[2, mm] = (dq_view[:, mm, kap] + xr[:, mm]).astype(BF16)
-    send_a2(2)
     send_b2(2)
 
-    for g, out in ((0, ov_ref), (1, ok_ref), (2, oq_ref)):
+    for g, out in enumerate((ov_ref, ok_ref, oq_ref)):
         wait_b(sb2.at[g], rb2.at[g], g, ss_b2, rs_b2)
         for j in range(NDP):
             scr[j * HALF:(j + 1) * HALF, :] = rb2[g, j][:HALF].astype(F32)
         rows = jnp.concatenate(
             [scr[pl.ds(h, ROWS, stride=HEADS), :].astype(BF16) for h in range(HEADS)], axis=1)
-        out[...] = jnp.dot(to_arrival, rows, preferred_element_type=F32).astype(BF16)
-
-    drain_b(sb_qk, rb_qk, 0, ss_b, rs_b)
-    drain_b(sb_1.at[0], rb_1.at[0], 1, ss_b, rs_b)
-    drain_b(sb_1.at[1], rb_1.at[1], 2, ss_b, rs_b)
-    for g in range(3):
-        drain_b(sb2.at[g], rb2.at[g], g, ss_b2, rs_b2)
-
-    def drain_m(e, c):
-        for arr in range(4):
-            copy_a(arr, m_peer(e)).wait_send()
-        for g in range(3):
-            copy_a2(g, m_peer(e)).wait_send()
-        return c
-
-    lax.fori_loop(1, NM, drain_m, 0)
-
-    def drain_f(e, c):
-        for a in range(2):
-            copy_f(a, e, kap).wait_send()
-        return c
-
-    lax.fori_loop(0, NM, drain_f, 0)
-    swap.wait_send()
+        done[g] = jnp.dot(to_arrival, rows, preferred_element_type=F32).astype(BF16)
+        store = pltpu.make_async_copy(done.at[g], out, out_sem.at[g])
+        store.start()
+        drains.append(store.wait)
+
+    for drain in drains:
+        drain()
 
 
 def local(queries, keys, values, gates, attn_out, grad_out, route, lengths):
-    vmem = pl.BlockSpec(memory_space=pltpu.VMEM)
+    hbm = pl.BlockSpec(memory_space=pl.ANY)
     smem = pl.BlockSpec(memory_space=pltpu.SMEM)
     dma = pltpu.SemaphoreType.DMA
     shape = jax.ShapeDtypeStruct((ROWS, D), BF16)
@@ -392,9 +409,11 @@
         kernel,
         name="hstu_backward",
         out_shape=[shape] * 4,
-        in_specs=[smem] * 2 + [vmem] * 6,
-        out_specs=[vmem] * 4,
+        in_specs=[smem] * 2 + [hbm] * 6,
+        out_specs=[hbm] * 4,
         scratch_shapes=[
+            pltpu.VMEM((6, ROWS, D), BF16),
+            pltpu.VMEM((4, ROWS, D), BF16),
             pltpu.VMEM((ROWS * 16, HD), F32),
             pltpu.VMEM((NDP, ROWS, HD), BF16),
             pltpu.VMEM((NDP, ROWS, HD), BF16),
@@ -403,9 +422,9 @@
             pltpu.VMEM((4, NM, 2, PADH, HD), BF16),
             pltpu.VMEM((2, 2, NCTX, PADH, HD), BF16),
             pltpu.VMEM((2, 2, NM, PADH, HD), BF16),
-            pltpu.VMEM((NRT, NPB, RT, PB), BF16),
-            pltpu.VMEM((NRT, NPB, RT, PB), F32),
-            pltpu.VMEM((NRT, NPB, RT, PB), BF16),
+            pltpu.VMEM((NRT, RT, NPB * PB), BF16),
+            pltpu.VMEM((NRT, RT, NPB * PB), F32),
+            pltpu.VMEM((NRT, RT, NPB * PB), BF16),
             pltpu.VMEM((NPB * PB, HD), F32),
             pltpu.VMEM((2, NM, PADH, HD), F32),
             pltpu.VMEM((2, NM, PADH, HD), F32),
@@ -413,10 +432,12 @@
             pltpu.VMEM((3, NM, 2, PADH, HD), BF16),
             pltpu.VMEM((3, NDP, PADH, HD), BF16),
             pltpu.VMEM((3, NDP, PADH, HD), BF16),
+            pltpu.VMEM((2, 8, NPB * PB), jnp.int32),
+            dma((6,)), dma((4,)),
             dma((3, NDP)), dma((3, NDP)),
             dma((4, NM)), dma((4, NM)),
             dma((2, NM)), dma((2, NM)),
-            dma, dma,
+            dma((2,)), dma((2,)),
             dma((3, NM)), dma((3, NM)),
             dma((3, NDP)), dma((3, NDP)),
         ],

time: 132 us -> 93.1 us (0.71)
  Pallas kernels: 126 us -> 87.3 us
    pallas_call x1, Pallas kernels: 126 us -> 87.3 us  [local(): pl.pallas_call(kernel, name='hstu_backward', out_shape=[shape] * 4, in_sp...]
where the time goes in v2:
time: 93.1 us; the launch traced here: 92.5 us
  Pallas kernels  87.3 us (94%)
  local copies, waits for them, and re-layouts  4.59 us (5%)
    pallas_call x1, Pallas kernels, local(): pl.pallas_call(kernel, name='hstu_backward', out_shape=[shape] * 4, in_sp...  87.3 us
    unnamed x10, local copies, waits for them, and re-layouts  4.59 us

profile of v2, /device:TPU:24, one launch (start us, length us, event | category | flops | bytes accessed | tf_op | source)
XLA Modules:
  0.0 92.5 jit_solution(3023785049450405494)
XLA Ops:
  0.6 87.3 %hstu_backward.1 = (bf16[144,1024]{1,0:T(8,128)(2,1)}, bf16[144,1024]{1,0:T(8,128)(2,1)}, bf16[144,1024]{1,0:T(8,128)(2,1)}, bf16[144,1024]{1,0:T(8,128)(2,1)}) custom-call(s32[1,16]{1,0:T(1,128)} %tgt.1, s32[1,4]{1,0:T(1,128)} %lens.1, bf16[144,1024]{1,0:T(8,128)(2,1)} %bitcast.14, bf16[144,1024]{1,0:T(8,128)(2,1)} %bitcast.15, bf16[144,1024]{1,0:T(8,128)(2,1)} %bitcast.16, ...), custom_call_target="tpu_custom_call" | custom-call | flops 3400000000 | bytes 3000000 | tf_op jit(solution)/shard_map/hstu_backward/pallas_call | solution.py:408
  87.9 0.0 copy-start.2
  87.9 1.7 %copy.16 = bf16[1,144,1024]{2,1,0:T(8,128)(2,1)} copy(bf16[1,144,1024]{2,1,0:T(8,128)(2,1)} %bitcast.13) | data formatting | bytes 589824
  89.6 0.0 copy-done.2
  89.6 0.0 copy-start.1
  89.6 0.7 copy.17
  90.4 0.4 copy-done.1
  90.7 0.0 copy-start
  90.7 0.7 copy.18
  91.4 0.4 copy-done
  91.8 0.7 copy.19
Async XLA Ops:
  87.9 1.8 %copy-start.2 = (bf16[144,1024]{1,0:T(8,128)(2,1)S(1)}, bf16[144,1024]{1,0:T(8,128)(2,1)}, u32[]{:S(2)}) copy-start(bf16[144,1024]{1,0:T(8,128)(2,1)} %get-tuple-element.9) | copy-start | bytes 884740
  89.6 1.1 %copy-start.1 = (bf16[144,1024]{1,0:T(8,128)(2,1)S(1)}, bf16[144,1024]{1,0:T(8,128)(2,1)}, u32[]{:S(2)}) copy-start(bf16[144,1024]{1,0:T(8,128)(2,1)} %get-tuple-element.10) | copy-start | bytes 884740
  90.7 1.1 %copy-start = (bf16[144,1024]{1,0:T(8,128)(2,1)S(1)}, bf16[144,1024]{1,0:T(8,128)(2,1)}, u32[]{:S(2)}) copy-start(bf16[144,1024]{1,0:T(8,128)(2,1)} %get-tuple-element.11) | copy-start | bytes 884740

commit v3 on v2

v3 whole, which is shorter than its diff:
```python
import math

import jax
import jax.numpy as jnp
from jax import lax
from jax.experimental import pallas as pl
from jax.experimental.pallas import tpu as pltpu
from jax.sharding import PartitionSpec as P

D = 1024
HEADS = 8
HD = 128
ROWS = 144
HALF = 72
PADH = 80
BLK = 9
NDP = 16
NZ = 8
NCTX = 16
NM = 8
USERS = 4
ATT_DIV = 32
RT = 160
PB = 256
NRT = 8
NPB = 10
NXY = 16
NB = 2 * BLK * HEADS
MESH = pl.DeviceIdType.MESH
F32 = jnp.float32
BF16 = jnp.bfloat16
NT = (((1,), (1,)), ((), ()))

GROUPS = ((0, 4, 0, 32), (4, 9, 32, 80))
WHOLE = (0, PADH)
PARTS = ((0, 32), (32, 80))
B_PARTS = ((0, 64), (64, NB))


def p_blocks(rt):
    return (rt, NPB) if rt < 4 else (5, 7 + rt - 4)


def inner_place(x):
    y = x - 32
    block = (y * 205) // 1024
    return jnp.where(x < 32, (x // 4) * BLK + x % 4, block * BLK + 4 + y - 5 * block)


def one_hots(tgt):
    row = lax.broadcasted_iota(jnp.int32, (ROWS, ROWS), 0)
    col = lax.broadcasted_iota(jnp.int32, (ROWS, ROWS), 1)
    shift_c = jnp.zeros((ROWS, ROWS), jnp.int32)
    shift_r = jnp.zeros((ROWS, ROWS), jnp.int32)
    for b in range(NDP):
        by = (tgt[0, b] - b) * BLK
        shift_c = jnp.where((col >= b * BLK) & (col < b * BLK + BLK), by, shift_c)
        shift_r = jnp.where((row >= b * BLK) & (row < b * BLK + BLK), by, shift_r)
    to_stream = jnp.where(row == col + shift_c, 1.0, 0.0).astype(BF16)
    to_arrival = jnp.where(col == row + shift_r, 1.0, 0.0).astype(BF16)
    return to_stream, to_arrival


def unpack(blocks, scr, to_arrival):
    for other in range(NZ):
        x = blocks[other].astype(F32)
        for stream in range(2):
            at = (stream * NZ + other) * HALF
            scr[at:at + 32, :] = x[stream * 32:stream * 32 + 32]
            scr[at + 32:at + HALF, :] = x[64 + stream * 40:104 + stream * 40]
    rows = jnp.concatenate(
        [scr[pl.ds(h, ROWS, stride=HEADS), :].astype(BF16) for h in range(HEADS)], axis=1)
    return jnp.dot(to_arrival, rows, preferred_element_type=F32).astype(BF16)


def kernel(
    tgt, lens, q_ref, k_ref, v_ref, u_ref, o_ref, dy_ref,
    oq_ref, ok_ref, ov_ref, ou_ref,
    held, done, scr, sb, rb, sa, qd, kv, kt, w_buf, f_buf, ds_buf,
    dq_buf, xs, xr, g2, r2, sb2, rb2, at_query,
    in_sem, out_sem, sent, rs_b, rs_a, rs_f, rs_x, rs_a2, rs_b2,
):
    dp = lax.axis_index("dp")
    ctx = lax.axis_index("ctx")
    xlo, z = dp // NZ, dp % NZ
    m, kap = ctx // 2, ctx % 2
    scale = 1.0 / math.sqrt(HD)
    twin = (dp, m * 2 + 1 - kap)

    def z_peer(d):
        return (z + d) % NZ

    def at_z(other):
        return (xlo * NZ + other, ctx)

    def xy_peer(e):
        return ((xlo + e) % 2) * NM + (m + e // 2) % NM

    def at_xy(unit):
        return ((unit // NM) * NZ + z, (unit % NM) * 2 + kap)

    mine = xlo * NM + m

    def loop(lo, hi, body):
        def step(i, c):
            body(i)
            return c

        lax.fori_loop(lo, hi, step, 0)

    loads = [
        pltpu.make_async_copy(ref, held.at[n], in_sem.at[n])
        for n, ref in enumerate((q_ref, k_ref, o_ref, dy_ref, u_ref, v_ref))
    ]
    for load in loads:
        load.start()

    barrier = pltpu.get_barrier_semaphore()
    loop(1, NZ, lambda d: pl.semaphore_signal(
        barrier, inc=1, device_id=at_z(z_peer(d)), device_id_type=MESH))
    loop(1, NXY, lambda e: pl.semaphore_signal(
        barrier, inc=1, device_id=at_xy(xy_peer(e)), device_id_type=MESH))
    pl.semaphore_signal(barrier, inc=1, device_id=twin, device_id_type=MESH)

    to_stream, to_arrival = one_hots(tgt)

    def pack_b(arrays, lo):
        n = len(arrays) * HEADS
        for a, x in enumerate(arrays):
            y = jnp.dot(to_stream, x, preferred_element_type=F32)
            for h in range(HEADS):
                scr[pl.ds(a * HEADS + h, ROWS, stride=n), :] = y[:, h * HD:(h + 1) * HD]
        for other in range(NZ):
            pieces = []
            for first, last, _, _ in GROUPS:
                for stream in range(2):
                    at = (stream * NZ + other) * BLK * n
                    pieces.append(scr[at + first * n:at + last * n, :])
            sb[other, lo:lo + 2 * BLK * n] = jnp.concatenate(pieces, axis=0).astype(BF16)

    def send_b(src, dst, lo, hi, send_sem, recv_sem):
        rows = pl.ds(lo, hi - lo)

        def step(d):
            other = z_peer(d)
            pltpu.make_async_remote_copy(
                src_ref=src.at[other, rows], dst_ref=dst.at[z, rows], send_sem=send_sem, recv_sem=recv_sem,
                device_id=at_z(other), device_id_type=MESH).start()

        loop(1, NZ, step)

    def wait_b(src, dst, lo, hi, send_sem, recv_sem):
        part = (pl.ds(0, NZ - 1), pl.ds(lo, hi - lo))
        pltpu.make_async_remote_copy(
            src_ref=src.at[part], dst_ref=dst.at[part], send_sem=send_sem, recv_sem=recv_sem,
            device_id=at_z(z_peer(1)), device_id_type=MESH).wait_recv()

    zeros8 = jnp.zeros((8, HD), F32)

    def pack_a(lo, arrays, group):
        n = len(arrays) * HEADS
        first, last, at, end = group
        r = last - first
        base = lo + 2 * first * n
        for other in range(NZ):
            x = rb[other, base:base + 2 * r * n].astype(F32)
            for stream in range(2):
                at_scr = (stream * NZ + other) * r * n
                scr[at_scr:at_scr + r * n, :] = x[stream * r * n:(stream + 1) * r * n]
        for a, arr in enumerate(arrays):
            for h in range(HEADS):
                x = scr[pl.ds(a * HEADS + h, NDP * r, stride=n), :]
                for stream in range(2):
                    y = x[stream * 8 * r:(stream + 1) * 8 * r]
                    if end - at > 8 * r:
                        y = jnp.concatenate([y, zeros8], axis=0)
                    sa[arr, stream * NM + h, at:end] = y.astype(BF16)

    def slot_a(arr, rows):
        return qd.at[arr // 2, xlo, ctx, rows] if arr % 2 == 0 else kv.at[arr // 2, xlo, m, rows]

    def send_a(arr, lo, hi, recv_sem):
        rows = pl.ds(lo, hi - lo)

        def step(e):
            unit = xy_peer(e)
            pltpu.make_async_remote_copy(
                src_ref=sa.at[arr, unit, rows], dst_ref=slot_a(arr, rows), send_sem=sent.at[1], recv_sem=recv_sem,
                device_id=at_xy(unit), device_id_type=MESH).start()

        loop(1, NXY, step)
        if arr % 2 == 0:
            qd[arr // 2, xlo, ctx, rows] = sa[arr, mine, rows]
        else:
            kv[arr // 2, xlo, m, rows] = sa[arr, mine, rows]

    def wait_a(arr, lo, hi, recv_sem):
        part = sa.at[arr, pl.ds(0, NXY - 1), pl.ds(lo, hi - lo)]
        pltpu.make_async_remote_copy(
            src_ref=part, dst_ref=part, send_sem=sent.at[1], recv_sem=recv_sem,
            device_id=at_xy(xy_peer(1)), device_id_type=MESH).wait_recv()

    def share(a):
        def step(mm):
            ref = qd.at[a, :, mm * 2 + kap]
            pltpu.make_async_remote_copy(
                src_ref=ref, dst_ref=ref, send_sem=sent.at[2], recv_sem=rs_f.at[a],
                device_id=twin, device_id_type=MESH).start()

        loop(0, NM, step)

    def wait_share(a):
        part = qd.at[a, :, pl.ds(0, NM)]
        pltpu.make_async_remote_copy(
            src_ref=part, dst_ref=part, send_sem=sent.at[2], recv_sem=rs_f.at[a],
            device_id=twin, device_id_type=MESH).wait_recv()

    def send_a2(g, lo, hi, recv_sem):
        rows = pl.ds(lo, hi - lo)

        def step(e):
            unit = xy_peer(e)
            pltpu.make_async_remote_copy(
                src_ref=g2.at[g, unit, rows], dst_ref=r2.at[g, mine, rows], send_sem=sent.at[4], recv_sem=recv_sem,
                device_id=at_xy(unit), device_id_type=MESH).start()

        loop(1, NXY, step)
        r2[g, mine, rows] = g2[g, mine, rows]

    def send_b2(g, lo, hi, from_sem, dst, recv_sem):
        part = r2.at[g, pl.ds(0, NXY - 1), pl.ds(lo, hi - lo)]
        pltpu.make_async_remote_copy(
            src_ref=part, dst_ref=part, send_sem=sent.at[4], recv_sem=from_sem,
            device_id=at_xy(xy_peer(1)), device_id_type=MESH).wait_recv()
        for first, last, at, end in GROUPS:
            if lo <= at < hi:
                r = last - first
                n = r * HEADS
                for stream in range(2):
                    for h in range(HEADS):
                        scr[pl.ds(stream * NZ * n + h, 8 * r, stride=HEADS), :] = (
                            r2[g, stream * NM + h, at:end].astype(F32)[:8 * r])
                for other in range(NZ):
                    sb2[g, other, 2 * at:2 * at + 2 * n] = jnp.concatenate(
                        [scr[(stream * NZ + other) * n:(stream * NZ + other + 1) * n, :] for stream in range(2)],
                        axis=0).astype(BF16)
        low, high = 2 * lo, min(2 * hi, NB)
        send_b(sb2.at[g], dst, low, high, sent.at[5], recv_sem)

    loads[0].wait()
    loads[1].wait()
    pack_b([held[0], held[1]], 0)
    pl.semaphore_wait(barrier, NZ - 1 + NXY - 1 + 1)
    b_qk = (sb, rb, 0, 2 * NB, sent.at[0], rs_b.at[0])
    send_b(*b_qk)
    rb[z, :2 * NB] = sb[z, :2 * NB]

    for load in loads[2:5]:
        load.wait()
    o_full = held[2].astype(F32)
    centred = o_full - jnp.mean(o_full, axis=1, keepdims=True)
    inv_std = 1.0 / jnp.sqrt(jnp.mean(centred * centred, axis=1, keepdims=True) + 1e-05)
    normed = centred * inv_std
    dy_full = held[3].astype(F32)
    done[3] = (dy_full * normed).astype(BF16)
    stores = [pltpu.make_async_copy(done.at[3], ou_ref, out_sem.at[3])]
    stores[0].start()
    g_term = dy_full * held[4].astype(F32)
    d_o = inv_std * (
        g_term
        - jnp.mean(g_term, axis=1, keepdims=True)
        - normed * jnp.mean(g_term * normed, axis=1, keepdims=True)
    )
    at_do, at_v = 2 * NB, 3 * NB
    pack_b([d_o.astype(BF16)], at_do)
    b_do = (sb, rb, at_do, at_do + NB, sent.at[0], rs_b.at[1])
    send_b(*b_do)
    loads[5].wait()
    pack_b([held[5]], at_v)
    b_v = [(sb, rb, at_v + lo, at_v + hi, sent.at[0], rs_b.at[2 + n]) for n, (lo, hi) in enumerate(B_PARTS)]
    for part in b_v:
        send_b(*part)
    rb[z, at_do:] = sb[z, at_do:]

    ends = []
    total = jnp.int32(0)
    for user in range(USERS):
        total = total + lens[0, user]
        ends.append(total)
    lane = lax.broadcasted_iota(jnp.int32, (8, NPB * PB), 1)
    late = lane >= NCTX * PADH
    lane_in = lane - jnp.where(late, NCTX * PADH, 0)
    chunk = jnp.zeros_like(lane_in)
    for c in range(1, NCTX):
        chunk = chunk + jnp.where(lane_in >= c * PADH, 1, 0)
    place = jnp.where(late, 2 * NCTX - 1 - chunk, chunk) * HALF + inner_place(lane_in - chunk * PADH)
    first = jnp.zeros_like(place)
    for user in range(USERS - 1):
        first = jnp.maximum(first, jnp.where(ends[user] <= place, ends[user], 0))
    at_query[0] = place
    at_query[1] = first

    sub = lax.broadcasted_iota(jnp.int32, (RT, PB), 0)
    second = jnp.where(sub >= PADH, 1, 0)
    key_inner = inner_place(sub - second * PADH)

    def key_places(rt):
        c = 2 * (2 * (rt % 4) + second) + kap
        return (c if rt < 4 else 2 * NCTX - 1 - c) * HALF + key_inner

    def q_at(a, lo, hi):
        return qd.at[a].reshape(2 * NCTX * PADH, HD)[lo * PB:hi * PB, :]

    def k_at(a, rt):
        return kv.at[a].reshape(2 * NM * PADH, HD)[rt * RT:(rt + 1) * RT, :]

    wait_b(*b_qk)
    for group in GROUPS:
        pack_a(0, [0, 1], group)
    send_a(0, *WHOLE, rs_a.at[0])
    send_a(1, *WHOLE, rs_a.at[1])

    wait_b(*b_do)
    for group in GROUPS:
        pack_a(at_do, [2], group)
    send_a(2, *WHOLE, rs_a.at[2])
    wait_a(0, *WHOLE, rs_a.at[0])
    share(0)

    wait_b(*b_v[0])
    pack_a(at_v, [3], GROUPS[0])
    send_a(3, *PARTS[0], rs_a.at[3])

    wait_b(*b_v[1])
    pack_a(at_v, [3], GROUPS[1])
    send_a(3, *PARTS[1], rs_a.at[4])

    wait_a(1, *WHOLE, rs_a.at[1])
    wait_share(0)

    for rt in range(NRT):
        keys = k_at(0, rt)
        kt[rt] = keys.T
        key_place = key_places(rt)
        for b in range(*p_blocks(rt)):
            at = slice(b * PB, (b + 1) * PB)
            s = lax.dot_general(keys, q_at(0, b, b + 1), NT, preferred_element_type=F32) * scale
            sig = 0.5 * jnp.tanh(0.5 * s) + 0.5
            live = (key_place <= at_query[0, :1, at]) & (key_place >= at_query[1, :1, at])
            sig = jnp.where(live, sig, 0.0)
            w = s * sig
            w_buf[rt, :, at] = w.astype(BF16)
            f_buf[rt, :, at] = sig * (1.0 - w) + w

    wait_a(2, *WHOLE, rs_a.at[2])
    share(1)
    wait_share(1)

    def put_keys_grad(g, rt, value):
        t, half = rt % 4, rt // 4
        g2[g, half * NM + 2 * t] = value[:PADH].astype(BF16)
        g2[g, half * NM + 2 * t + 1] = value[PADH:].astype(BF16)

    for rt in range(NRT):
        lo, hi = p_blocks(rt)
        acc = jnp.dot(w_buf[rt, :, lo * PB:hi * PB], q_at(1, lo, hi), preferred_element_type=F32)
        put_keys_grad(0, rt, acc * (1.0 / ATT_DIV))
    for n, part in enumerate(PARTS):
        send_a2(0, *part, rs_a2.at[n])

    for n, part in enumerate(PARTS):
        wait_a(3, *part, rs_a.at[3 + n])
    for rt in range(NRT):
        values = k_at(1, rt)
        lo, hi = p_blocks(rt)
        for b in range(lo, hi):
            at = slice(b * PB, (b + 1) * PB)
            dw = lax.dot_general(values, q_at(1, b, b + 1), NT, preferred_element_type=F32)
            ds_buf[rt, :, at] = (dw * f_buf[rt, :, at]).astype(BF16)
        acc = jnp.dot(ds_buf[rt, :, lo * PB:hi * PB], q_at(0, lo, hi), preferred_element_type=F32)
        put_keys_grad(1, rt, acc * (scale / ATT_DIV))
    send_a2(1, *WHOLE, rs_a2.at[2])
    for n, part in enumerate(PARTS):
        send_b2(0, *part, rs_a2.at[n], rb2.at[0], rs_b2.at[n])
    rb2[0, z] = sb2[0, z]

    dq_view = dq_buf.reshape(2, NM, 2, PADH, HD)

    def swap(half):
        return pltpu.make_async_remote_copy(
            src_ref=xs.at[half], dst_ref=xr.at[half], send_sem=sent.at[3], recv_sem=rs_x.at[half],
            device_id=twin, device_id_type=MESH)

    for half in range(2):
        for b in range(half * NPB // 2, (half + 1) * NPB // 2):
            acc = jnp.zeros((HD, PB), F32)
            for rt in range(NRT):
                lo, hi = p_blocks(rt)
                if lo <= b < hi:
                    acc = acc + jnp.dot(
                        kt[rt], ds_buf[rt, :, b * PB:(b + 1) * PB], preferred_element_type=F32)
            dq_buf[b * PB:(b + 1) * PB, :] = acc.T * (scale / ATT_DIV)
        xs[half] = dq_view[half, :, 1 - kap]
        swap(half).start()
    for half in range(2):
        swap(half).wait_recv()
        for mm in range(NM):
            g2[2, half * NM + mm] = (dq_view[half, mm, kap] + xr[half, mm]).astype(BF16)
    send_a2(2, *WHOLE, rs_a2.at[3])
    send_b2(1, *WHOLE, rs_a2.at[2], rb2.at[1], rs_b2.at[2])
    rb2[1, z] = sb2[1, z]
    send_b2(2, *WHOLE, rs_a2.at[3], oq_ref, rs_b2.at[3])
    keep = pltpu.make_async_copy(sb2.at[2, z], oq_ref.at[z], out_sem.at[2])
    keep.start()
    stores.append(keep)

    homes = (
        [(sb2.at[0], rb2.at[0], *part, sent.at[5], rs_b2.at[n]) for n, part in enumerate(B_PARTS)],
        [(sb2.at[1], rb2.at[1], 0, NB, sent.at[5], rs_b2.at[2])],
    )
    for g, out in enumerate((ov_ref, ok_ref)):
        for home in homes[g]:
            wait_b(*home)
        done[g] = unpack(rb2.at[g], scr, to_arrival)
        stores.append(pltpu.make_async_copy(done.at[g], out, out_sem.at[g]))
        stores[-1].start()
    wait_b(sb2.at[2], oq_ref, 0, NB, sent.at[5], rs_b2.at[3])

    for n, part in enumerate((
        sb.at[pl.ds(0, NZ - 1)], sa.at[:, pl.ds(0, NXY - 1)], qd.at[:, :, pl.ds(0, NM)], xs,
        g2.at[:, pl.ds(0, NXY - 1)], sb2.at[:, pl.ds(0, NZ - 1)],
    )):
        pltpu.make_async_remote_copy(
            src_ref=part, dst_ref=part, send_sem=sent.at[n], recv_sem=rs_x.at[0],
            device_id=twin, device_id_type=MESH).wait_send()
    for store in stores:
        store.wait()


def finish(tgt, q_ref, k_ref, v_ref, u_ref, oq_ref, ok_ref, ov_ref, ou_ref, blocks, rows, scr, sems):
    ins = [pltpu.make_async_copy(q_ref, blocks, sems.at[0])]
    outs = []
    for n, (ref, out) in enumerate(((k_ref, ok_ref), (v_ref, ov_ref), (u_ref, ou_ref))):
        ins.append(pltpu.make_async_copy(ref, rows.at[n], sems.at[n + 1]))
        outs.append(pltpu.make_async_copy(rows.at[n], out, sems.at[n + 4]))
    for copy in ins:
        copy.start()
    _, to_arrival = one_hots(tgt)
    ins[0].wait()
    rows[3] = unpack(blocks, scr, to_arrival)
    outs.append(pltpu.make_async_copy(rows.at[3], oq_ref, sems.at[7]))
    outs[3].start()
    for n in range(3):
        ins[n + 1].wait()
        outs[n].start()
    for copy in outs:
        copy.wait()


def local(queries, keys, values, gates, attn_out, grad_out, route, lengths):
    hbm = pl.BlockSpec(memory_space=pl.ANY)
    smem = pl.BlockSpec(memory_space=pltpu.SMEM)
    dma = pltpu.SemaphoreType.DMA
    shape = jax.ShapeDtypeStruct((ROWS, D), BF16)
    attention = (NRT, RT, NPB * PB)
    outs = pl.pallas_call(
        kernel,
        name="hstu_backward",
        out_shape=[jax.ShapeDtypeStruct((NZ, NB, HD), BF16)] + [shape] * 3,
        in_specs=[smem] * 2 + [hbm] * 6,
        out_specs=[hbm] * 4,
        scratch_shapes=[
            pltpu.VMEM((6, ROWS, D), BF16),
            pltpu.VMEM((4, ROWS, D), BF16),
            pltpu.VMEM((ROWS * 16, HD), F32),
            pltpu.VMEM((NZ, 4 * NB, HD), BF16),
            pltpu.VMEM((NZ, 4 * NB, HD), BF16),
            pltpu.VMEM((4, NXY, PADH, HD), BF16),
            pltpu.VMEM((2, 2, NCTX, PADH, HD), BF16),
            pltpu.VMEM((2, 2, NM, PADH, HD), BF16),
            pltpu.VMEM((NRT, HD, RT), BF16),
            pltpu.VMEM(attention, BF16),
            pltpu.VMEM(attention, F32),
            pltpu.VMEM(attention, BF16),
            pltpu.VMEM((NPB * PB, HD), F32),
            pltpu.VMEM((2, NM, PADH, HD), F32),
            pltpu.VMEM((2, NM, PADH, HD), F32),
            pltpu.VMEM((3, NXY, PADH, HD), BF16),
            pltpu.VMEM((3, NXY, PADH, HD), BF16),
            pltpu.VMEM((3, NZ, NB, HD), BF16),
            pltpu.VMEM((2, NZ, NB, HD), BF16),
            pltpu.VMEM((2, 8, NPB * PB), jnp.int32),
            dma((6,)), dma((4,)), dma((6,)),
            dma((4,)), dma((5,)), dma((2,)), dma((2,)), dma((4,)), dma((4,)),
        ],
        compiler_params=pltpu.CompilerParams(
            collective_id=0, has_side_effects=True, vmem_limit_bytes=56 * 1024 * 1024
        ),
        cost_estimate=pl.CostEstimate(flops=3_400_000_000, bytes_accessed=3_000_000, transcendentals=2_000_000),
    )(route, lengths, queries[0], keys[0], values[0], gates[0], attn_out[0], grad_out[0])
    outs = pl.pallas_call(
        finish,
        name="finish",
        out_shape=[shape] * 4,
        in_specs=[smem] + [hbm] * 4,
        out_specs=[hbm] * 4,
        scratch_shapes=[
            pltpu.VMEM((NZ, NB, HD), BF16),
            pltpu.VMEM((4, ROWS, D), BF16),
            pltpu.VMEM((ROWS * HEADS, HD), F32),
            dma((8,)),
        ],
        compiler_params=pltpu.CompilerParams(vmem_limit_bytes=56 * 1024 * 1024),
    )(route, *outs)
    return tuple(x[None] for x in outs)


def solution(mesh):
    rows = P("dp", "ctx", None)
    return jax.shard_map(
        local,
        mesh=mesh,
        in_specs=(rows,) * 6 + (P("dp", "ctx"), P("dp", None)),
        out_specs=(rows,) * 4,
        check_vma=False,
    )
```

time: 93.1 us -> 76.8 us (0.82)
  Pallas kernels: 87.3 us -> 74.7 us
  local copies, waits for them, and re-layouts: 4.59 us -> 0 us
    pallas_call x1 -> x2, Pallas kernels: 87.3 us -> 74.7 us  [the longest x1 71.7 us: local(): pl.pallas_call(kernel, name='hstu_backward', out_shape=[jax.ShapeDtypeStr...]
    unnamed x10 -> x0, local copies, waits for them, and re-layouts: 4.59 us -> none
where the time goes in v3:
time: 76.8 us; the launch traced here: 75.4 us
  Pallas kernels  74.7 us (97%)
    pallas_call x1, Pallas kernels, local(): pl.pallas_call(kernel, name='hstu_backward', out_shape=[jax.ShapeDtypeStr...  71.7 us
    pallas_call x1, Pallas kernels, local(): pl.pallas_call(finish, name='finish', out_shape=[shape] * 4, in_specs=[sm...  2.99 us

profile of v3, /device:TPU:24, one launch (start us, length us, event | category | flops | bytes accessed | tf_op | source)
XLA Modules:
  0.0 75.4 jit_solution(4095162160997736183)
XLA Ops:
  0.6 71.7 %hstu_backward.1 = (bf16[8,144,128]{2,1,0:T(8,128)(2,1)}, bf16[144,1024]{1,0:T(8,128)(2,1)}, bf16[144,1024]{1,0:T(8,128)(2,1)}, bf16[144,1024]{1,0:T(8,128)(2,1)}) custom-call(s32[1,16]{1,0:T(1,128)} %tgt.3, s32[1,4]{1,0:T(1,128)} %lens.1, bf16[144,1024]{1,0:T(8,128)(2,1)} %bitcast.10, bf16[144,1024]{1,0:T(8,128)(2,1)} %bitcast.11, ...), custom_call_target="tpu_custom_call" | custom-call | flops 3400000000 | bytes 3000000 | tf_op jit(solution)/shard_map/hstu_backward/pallas_call | solution.py:466
  72.4 3.0 %finish.1 = (bf16[144,1024]{1,0:T(8,128)(2,1)}, bf16[144,1024]{1,0:T(8,128)(2,1)}, bf16[144,1024]{1,0:T(8,128)(2,1)}, bf16[144,1024]{1,0:T(8,128)(2,1)}) custom-call(s32[1,16]{1,0:T(1,128)} %tgt.3, bf16[8,144,128]{2,1,0:T(8,128)(2,1)} %get-tuple-element.12.q_ref, bf16[144,1024]{1,0:T(8,128)(2,1)} %get-tuple-element.13.k_ref, ...), custom_call_target="tpu_custom_call" | custom-call | tf_op jit(solution)/shard_map/finish/pallas_call | solution.py:501

commit v4 on v3

--- a/solution.py
+++ b/solution.py
@@ -35,6 +35,9 @@
 WHOLE = (0, PADH)
 PARTS = ((0, 32), (32, 80))
 B_PARTS = ((0, 64), (64, NB))
+IN_ONE = (((0, PADH), (0, NB), GROUPS),)
+IN_TWO = (((0, 32), (0, 64), GROUPS[:1]), ((32, PADH), (64, NB), GROUPS[1:]))
+CUT_QK, CUT_DO, CUT_V, CUT_DV, CUT_DK, CUT_DQ = IN_TWO, IN_ONE, IN_TWO, IN_TWO, IN_ONE, IN_ONE
 
 
 def p_blocks(rt):
@@ -76,7 +79,7 @@
 def kernel(
     tgt, lens, q_ref, k_ref, v_ref, u_ref, o_ref, dy_ref,
     oq_ref, ok_ref, ov_ref, ou_ref,
-    held, done, scr, sb, rb, sa, qd, kv, kt, w_buf, f_buf, ds_buf,
+    held, done, scr, sb, rb, sa, events, kt, w_buf, f_buf, ds_buf,
     dq_buf, xs, xr, g2, r2, sb2, rb2, at_query,
     in_sem, out_sem, sent, rs_b, rs_a, rs_f, rs_x, rs_a2, rs_b2,
 ):
@@ -88,16 +91,16 @@
     twin = (dp, m * 2 + 1 - kap)
 
     def z_peer(d):
-        return (z + d) % NZ
+        return lax.rem(z + d, NZ)
 
     def at_z(other):
         return (xlo * NZ + other, ctx)
 
     def xy_peer(e):
-        return ((xlo + e) % 2) * NM + (m + e // 2) % NM
+        return lax.rem(xlo + e, 2) * NM + lax.rem(m + lax.div(e, 2), NM)
 
     def at_xy(unit):
-        return ((unit // NM) * NZ + z, (unit % NM) * 2 + kap)
+        return (lax.div(unit, NM) * NZ + z, lax.rem(unit, NM) * 2 + kap)
 
     mine = xlo * NM + m
 
@@ -106,7 +109,7 @@
             body(i)
             return c
 
-        lax.fori_loop(lo, hi, step, 0)
+        lax.fori_loop(lo, hi, step, 0, unroll=True)
 
     loads = [
         pltpu.make_async_copy(ref, held.at[n], in_sem.at[n])
@@ -176,44 +179,29 @@
                         y = jnp.concatenate([y, zeros8], axis=0)
                     sa[arr, stream * NM + h, at:end] = y.astype(BF16)
 
-    def slot_a(arr, rows):
-        return qd.at[arr // 2, xlo, ctx, rows] if arr % 2 == 0 else kv.at[arr // 2, xlo, m, rows]
-
-    def send_a(arr, lo, hi, recv_sem):
-        rows = pl.ds(lo, hi - lo)
+    def send_a(arr, n, lo, hi, recv_sem):
+        arrs, rows = pl.ds(arr, n), pl.ds(lo, hi - lo)
 
         def step(e):
             unit = xy_peer(e)
             pltpu.make_async_remote_copy(
-                src_ref=sa.at[arr, unit, rows], dst_ref=slot_a(arr, rows), send_sem=sent.at[1], recv_sem=recv_sem,
-                device_id=at_xy(unit), device_id_type=MESH).start()
+                src_ref=sa.at[arrs, unit, rows], dst_ref=events.at[arrs, xlo, m, kap, rows],
+                send_sem=sent.at[1], recv_sem=recv_sem, device_id=at_xy(unit), device_id_type=MESH).start()
 
         loop(1, NXY, step)
-        if arr % 2 == 0:
-            qd[arr // 2, xlo, ctx, rows] = sa[arr, mine, rows]
-        else:
-            kv[arr // 2, xlo, m, rows] = sa[arr, mine, rows]
-
-    def wait_a(arr, lo, hi, recv_sem):
-        part = sa.at[arr, pl.ds(0, NXY - 1), pl.ds(lo, hi - lo)]
+        events[arrs, xlo, m, kap, rows] = sa[arrs, mine, rows]
+
+    def wait_a(arr, n, lo, hi, recv_sem):
+        part = sa.at[pl.ds(arr, n), pl.ds(0, NXY - 1), pl.ds(lo, hi - lo)]
         pltpu.make_async_remote_copy(
             src_ref=part, dst_ref=part, send_sem=sent.at[1], recv_sem=recv_sem,
-            device_id=at_xy(xy_peer(1)), device_id_type=MESH).wait_recv()
-
-    def share(a):
-        def step(mm):
-            ref = qd.at[a, :, mm * 2 + kap]
-            pltpu.make_async_remote_copy(
-                src_ref=ref, dst_ref=ref, send_sem=sent.at[2], recv_sem=rs_f.at[a],
-                device_id=twin, device_id_type=MESH).start()
-
-        loop(0, NM, step)
-
-    def wait_share(a):
-        part = qd.at[a, :, pl.ds(0, NM)]
-        pltpu.make_async_remote_copy(
-            src_ref=part, dst_ref=part, send_sem=sent.at[2], recv_sem=rs_f.at[a],
-            device_id=twin, device_id_type=MESH).wait_recv()
+            device_id=at_xy(xy_peer(jnp.int32(1))), device_id_type=MESH).wait_recv()
+
+    def share(arr, par, lo, hi, recv_sem):
+        ref = events.at[arr, :, :, par, pl.ds(lo, hi - lo)]
+        return pltpu.make_async_remote_copy(
+            src_ref=ref, dst_ref=ref, send_sem=sent.at[2], recv_sem=recv_sem,
+            device_id=twin, device_id_type=MESH)
 
     def send_a2(g, lo, hi, recv_sem):
         rows = pl.ds(lo, hi - lo)
@@ -231,7 +219,7 @@
         part = r2.at[g, pl.ds(0, NXY - 1), pl.ds(lo, hi - lo)]
         pltpu.make_async_remote_copy(
             src_ref=part, dst_ref=part, send_sem=sent.at[4], recv_sem=from_sem,
-            device_id=at_xy(xy_peer(1)), device_id_type=MESH).wait_recv()
+            device_id=at_xy(xy_peer(jnp.int32(1))), device_id_type=MESH).wait_recv()
         for first, last, at, end in GROUPS:
             if lo <= at < hi:
                 r = last - first
@@ -251,8 +239,9 @@
     loads[1].wait()
     pack_b([held[0], held[1]], 0)
     pl.semaphore_wait(barrier, NZ - 1 + NXY - 1 + 1)
-    b_qk = (sb, rb, 0, 2 * NB, sent.at[0], rs_b.at[0])
-    send_b(*b_qk)
+    b_qk = [(sb, rb, 2 * lo, 2 * hi, sent.at[0], rs_b.at[n]) for n, (_, (lo, hi), _) in enumerate(CUT_QK)]
+    for part in b_qk:
+        send_b(*part)
     rb[z, :2 * NB] = sb[z, :2 * NB]
 
     for load in loads[2:5]:
@@ -273,11 +262,12 @@
     )
     at_do, at_v = 2 * NB, 3 * NB
     pack_b([d_o.astype(BF16)], at_do)
-    b_do = (sb, rb, at_do, at_do + NB, sent.at[0], rs_b.at[1])
-    send_b(*b_do)
+    b_do = [(sb, rb, at_do + lo, at_do + hi, sent.at[0], rs_b.at[2 + n]) for n, (_, (lo, hi), _) in enumerate(CUT_DO)]
+    for part in b_do:
+        send_b(*part)
     loads[5].wait()
     pack_b([held[5]], at_v)
-    b_v = [(sb, rb, at_v + lo, at_v + hi, sent.at[0], rs_b.at[2 + n]) for n, (lo, hi) in enumerate(B_PARTS)]
+    b_v = [(sb, rb, at_v + lo, at_v + hi, sent.at[0], rs_b.at[4 + n]) for n, (_, (lo, hi), _) in enumerate(CUT_V)]
     for part in b_v:
         send_b(*part)
     rb[z, at_do:] = sb[z, at_do:]
@@ -309,34 +299,35 @@
         return (c if rt < 4 else 2 * NCTX - 1 - c) * HALF + key_inner
 
     def q_at(a, lo, hi):
-        return qd.at[a].reshape(2 * NCTX * PADH, HD)[lo * PB:hi * PB, :]
+        return events.at[2 * a].reshape(2 * NCTX * PADH, HD)[lo * PB:hi * PB, :]
 
     def k_at(a, rt):
-        return kv.at[a].reshape(2 * NM * PADH, HD)[rt * RT:(rt + 1) * RT, :]
-
-    wait_b(*b_qk)
-    for group in GROUPS:
-        pack_a(0, [0, 1], group)
-    send_a(0, *WHOLE, rs_a.at[0])
-    send_a(1, *WHOLE, rs_a.at[1])
-
-    wait_b(*b_do)
-    for group in GROUPS:
-        pack_a(at_do, [2], group)
-    send_a(2, *WHOLE, rs_a.at[2])
-    wait_a(0, *WHOLE, rs_a.at[0])
-    share(0)
-
-    wait_b(*b_v[0])
-    pack_a(at_v, [3], GROUPS[0])
-    send_a(3, *PARTS[0], rs_a.at[3])
-
-    wait_b(*b_v[1])
-    pack_a(at_v, [3], GROUPS[1])
-    send_a(3, *PARTS[1], rs_a.at[4])
-
-    wait_a(1, *WHOLE, rs_a.at[1])
-    wait_share(0)
+        half, t = rt // 4, rt % 4
+        return jnp.concatenate([events[2 * a + 1, half, 2 * t + n, kap] for n in range(2)], axis=0)
+
+    def get_b(parts, cut, n, lo, arrays):
+        rows, _, groups = cut[n]
+        wait_b(*parts[n])
+        for group in groups:
+            pack_a(lo, arrays, group)
+        send_a(arrays[0], len(arrays), *rows, rs_a.at[arrays[0], n])
+
+    def get_a(arr, count, cut):
+        for n, (rows, _, _) in enumerate(cut):
+            wait_a(arr, count, *rows, rs_a.at[arr, n])
+            if arr < 3:
+                share(arr, kap, *rows, rs_f.at[arr, n]).start()
+
+    def get_share(arr, cut):
+        for n, (rows, _, _) in enumerate(cut):
+            share(arr, 1 - kap, *rows, rs_f.at[arr, n]).wait_recv()
+
+    for n in range(len(CUT_QK)):
+        get_b(b_qk, CUT_QK, n, 0, [0, 1])
+    for n in range(len(CUT_DO)):
+        get_b(b_do, CUT_DO, n, at_do, [2])
+    get_a(0, 2, CUT_QK)
+    get_share(0, CUT_QK)
 
     for rt in range(NRT):
         keys = k_at(0, rt)
@@ -352,9 +343,10 @@
             w_buf[rt, :, at] = w.astype(BF16)
             f_buf[rt, :, at] = sig * (1.0 - w) + w
 
-    wait_a(2, *WHOLE, rs_a.at[2])
-    share(1)
-    wait_share(1)
+    get_b(b_v, CUT_V, 0, at_v, [3])
+    get_a(2, 1, CUT_DO)
+    get_b(b_v, CUT_V, 1, at_v, [3])
+    get_share(2, CUT_DO)
 
     def put_keys_grad(g, rt, value):
         t, half = rt % 4, rt // 4
@@ -365,11 +357,10 @@
         lo, hi = p_blocks(rt)
         acc = jnp.dot(w_buf[rt, :, lo * PB:hi * PB], q_at(1, lo, hi), preferred_element_type=F32)
         put_keys_grad(0, rt, acc * (1.0 / ATT_DIV))
-    for n, part in enumerate(PARTS):
-        send_a2(0, *part, rs_a2.at[n])
-
-    for n, part in enumerate(PARTS):
-        wait_a(3, *part, rs_a.at[3 + n])
+    for n, (rows, _, _) in enumerate(CUT_DV):
+        send_a2(0, *rows, rs_a2.at[0, n])
+
+    get_a(3, 1, CUT_V)
     for rt in range(NRT):
         values = k_at(1, rt)
         lo, hi = p_blocks(rt)
@@ -379,9 +370,10 @@
             ds_buf[rt, :, at] = (dw * f_buf[rt, :, at]).astype(BF16)
         acc = jnp.dot(ds_buf[rt, :, lo * PB:hi * PB], q_at(0, lo, hi), preferred_element_type=F32)
         put_keys_grad(1, rt, acc * (scale / ATT_DIV))
-    send_a2(1, *WHOLE, rs_a2.at[2])
-    for n, part in enumerate(PARTS):
-        send_b2(0, *part, rs_a2.at[n], rb2.at[0], rs_b2.at[n])
+    for n, (rows, _, _) in enumerate(CUT_DK):
+        send_a2(1, *rows, rs_a2.at[1, n])
+    for n, (rows, _, _) in enumerate(CUT_DV):
+        send_b2(0, *rows, rs_a2.at[0, n], rb2.at[0], rs_b2.at[0, n])
     rb2[0, z] = sb2[0, z]
 
     dq_view = dq_buf.reshape(2, NM, 2, PADH, HD)
@@ -406,28 +398,30 @@
         swap(half).wait_recv()
         for mm in range(NM):
             g2[2, half * NM + mm] = (dq_view[half, mm, kap] + xr[half, mm]).astype(BF16)
-    send_a2(2, *WHOLE, rs_a2.at[3])
-    send_b2(1, *WHOLE, rs_a2.at[2], rb2.at[1], rs_b2.at[2])
+    for n, (rows, _, _) in enumerate(CUT_DQ):
+        send_a2(2, *rows, rs_a2.at[2, n])
+    for n, (rows, _, _) in enumerate(CUT_DK):
+        send_b2(1, *rows, rs_a2.at[1, n], rb2.at[1], rs_b2.at[1, n])
     rb2[1, z] = sb2[1, z]
-    send_b2(2, *WHOLE, rs_a2.at[3], oq_ref, rs_b2.at[3])
+    for n, (rows, _, _) in enumerate(CUT_DQ):
+        send_b2(2, *rows, rs_a2.at[2, n], oq_ref, rs_b2.at[2, n])
     keep = pltpu.make_async_copy(sb2.at[2, z], oq_ref.at[z], out_sem.at[2])
     keep.start()
     stores.append(keep)
 
-    homes = (
-        [(sb2.at[0], rb2.at[0], *part, sent.at[5], rs_b2.at[n]) for n, part in enumerate(B_PARTS)],
-        [(sb2.at[1], rb2.at[1], 0, NB, sent.at[5], rs_b2.at[2])],
-    )
+    def home(g, cut, dst):
+        for n, (_, (lo, hi), _) in enumerate(cut):
+            wait_b(sb2.at[g], dst, lo, hi, sent.at[5], rs_b2.at[g, n])
+
     for g, out in enumerate((ov_ref, ok_ref)):
-        for home in homes[g]:
-            wait_b(*home)
+        home(g, (CUT_DV, CUT_DK)[g], rb2.at[g])
         done[g] = unpack(rb2.at[g], scr, to_arrival)
         stores.append(pltpu.make_async_copy(done.at[g], out, out_sem.at[g]))
         stores[-1].start()
-    wait_b(sb2.at[2], oq_ref, 0, NB, sent.at[5], rs_b2.at[3])
+    home(2, CUT_DQ, oq_ref)
 
     for n, part in enumerate((
-        sb.at[pl.ds(0, NZ - 1)], sa.at[:, pl.ds(0, NXY - 1)], qd.at[:, :, pl.ds(0, NM)], xs,
+        sb.at[pl.ds(0, NZ - 1)], sa.at[:, pl.ds(0, NXY - 1)], events.at[pl.ds(0, 2), :, :, 0], xs,
         g2.at[:, pl.ds(0, NXY - 1)], sb2.at[:, pl.ds(0, NZ - 1)],
     )):
         pltpu.make_async_remote_copy(
@@ -476,8 +470,7 @@
             pltpu.VMEM((NZ, 4 * NB, HD), BF16),
             pltpu.VMEM((NZ, 4 * NB, HD), BF16),
             pltpu.VMEM((4, NXY, PADH, HD), BF16),
-            pltpu.VMEM((2, 2, NCTX, PADH, HD), BF16),
-            pltpu.VMEM((2, 2, NM, PADH, HD), BF16),
+            pltpu.VMEM((4, 2, NM, 2, PADH, HD), BF16),
             pltpu.VMEM((NRT, HD, RT), BF16),
             pltpu.VMEM(attention, BF16),
             pltpu.VMEM(attention, F32),
@@ -491,7 +484,7 @@
             pltpu.VMEM((2, NZ, NB, HD), BF16),
             pltpu.VMEM((2, 8, NPB * PB), jnp.int32),
             dma((6,)), dma((4,)), dma((6,)),
-            dma((4,)), dma((5,)), dma((2,)), dma((2,)), dma((4,)), dma((4,)),
+            dma((6,)), dma((4, 2)), dma((3, 2)), dma((2,)), dma((3, 2)), dma((3, 2)),
         ],
         compiler_params=pltpu.CompilerParams(
             collective_id=0, has_side_effects=True, vmem_limit_bytes=56 * 1024 * 1024

time: 76.8 us -> 75.2 us (0.979)
  Pallas kernels: 74.7 us -> 73.5 us
    pallas_call x1, Pallas kernels: 71.7 us -> 70.6 us  [local(): pl.pallas_call(kernel, name='hstu_backward', out_shape=[jax.ShapeDtypeStr...]
where the time goes in v4:
time: 75.2 us; the launch traced here: 74.2 us
  Pallas kernels  73.5 us (98%)
    pallas_call x1, Pallas kernels, local(): pl.pallas_call(kernel, name='hstu_backward', out_shape=[jax.ShapeDtypeStr...  70.6 us
    pallas_call x1, Pallas kernels, local(): pl.pallas_call(finish, name='finish', out_shape=[shape] * 4, in_specs=[sm...  2.99 us

profile of v4, /device:TPU:24, one launch (start us, length us, event | category | flops | bytes accessed | tf_op | source)
XLA Modules:
  0.0 74.2 jit_solution(1648480371429427465)
XLA Ops:
  0.6 70.6 %hstu_backward.1 = (bf16[8,144,128]{2,1,0:T(8,128)(2,1)}, bf16[144,1024]{1,0:T(8,128)(2,1)}, bf16[144,1024]{1,0:T(8,128)(2,1)}, bf16[144,1024]{1,0:T(8,128)(2,1)}) custom-call(s32[1,16]{1,0:T(1,128)} %tgt.3, s32[1,4]{1,0:T(1,128)} %lens.1, bf16[144,1024]{1,0:T(8,128)(2,1)} %bitcast.10, bf16[144,1024]{1,0:T(8,128)(2,1)} %bitcast.11, ...), custom_call_target="tpu_custom_call" | custom-call | flops 3400000000 | bytes 3000000 | tf_op jit(solution)/shard_map/hstu_backward/pallas_call | solution.py:460
  71.2 3.0 %finish.1 = (bf16[144,1024]{1,0:T(8,128)(2,1)}, bf16[144,1024]{1,0:T(8,128)(2,1)}, bf16[144,1024]{1,0:T(8,128)(2,1)}, bf16[144,1024]{1,0:T(8,128)(2,1)}) custom-call(s32[1,16]{1,0:T(1,128)} %tgt.3, bf16[8,144,128]{2,1,0:T(8,128)(2,1)} %get-tuple-element.12.q_ref, bf16[144,1024]{1,0:T(8,128)(2,1)} %get-tuple-element.13.k_ref, ...), custom_call_target="tpu_custom_call" | custom-call | tf_op jit(solution)/shard_map/finish/pallas_call | solution.py:494

commit v5 on v4

--- a/solution.py
+++ b/solution.py
@@ -26,6 +26,7 @@
 NPB = 10
 NXY = 16
 NB = 2 * BLK * HEADS
+Z_STEPS = (4, 3, 5, 2, 6, 1, 7)
 MESH = pl.DeviceIdType.MESH
 F32 = jnp.float32
 BF16 = jnp.bfloat16
@@ -119,8 +120,8 @@
         load.start()
 
     barrier = pltpu.get_barrier_semaphore()
-    loop(1, NZ, lambda d: pl.semaphore_signal(
-        barrier, inc=1, device_id=at_z(z_peer(d)), device_id_type=MESH))
+    for d in Z_STEPS:
+        pl.semaphore_signal(barrier, inc=1, device_id=at_z(z_peer(d)), device_id_type=MESH)
     loop(1, NXY, lambda e: pl.semaphore_signal(
         barrier, inc=1, device_id=at_xy(xy_peer(e)), device_id_type=MESH))
     pl.semaphore_signal(barrier, inc=1, device_id=twin, device_id_type=MESH)
@@ -150,7 +151,8 @@
                 src_ref=src.at[other, rows], dst_ref=dst.at[z, rows], send_sem=send_sem, recv_sem=recv_sem,
                 device_id=at_z(other), device_id_type=MESH).start()
 
-        loop(1, NZ, step)
+        for d in Z_STEPS:
+            step(d)
 
     def wait_b(src, dst, lo, hi, send_sem, recv_sem):
         part = (pl.ds(0, NZ - 1), pl.ds(lo, hi - lo))

time: 75.2 us -> 74.3 us (0.988)
  no operation moved by 1% of the time
where the time goes in v5:
time: 74.3 us; the launch traced here: 73.5 us
  Pallas kernels  72.9 us (98%)
    pallas_call x1, Pallas kernels, local(): pl.pallas_call(kernel, name='hstu_backward', out_shape=[jax.ShapeDtypeStr...  69.9 us
    pallas_call x1, Pallas kernels, local(): pl.pallas_call(finish, name='finish', out_shape=[shape] * 4, in_specs=[sm...  2.99 us

profile of v5, /device:TPU:24, one launch (start us, length us, event | category | flops | bytes accessed | tf_op | source)
XLA Modules:
  0.0 73.5 jit_solution(9983403302433508432)
XLA Ops:
  0.6 69.9 %hstu_backward.1 = (bf16[8,144,128]{2,1,0:T(8,128)(2,1)}, bf16[144,1024]{1,0:T(8,128)(2,1)}, bf16[144,1024]{1,0:T(8,128)(2,1)}, bf16[144,1024]{1,0:T(8,128)(2,1)}) custom-call(s32[1,16]{1,0:T(1,128)} %tgt.3, s32[1,4]{1,0:T(1,128)} %lens.1, bf16[144,1024]{1,0:T(8,128)(2,1)} %bitcast.10, bf16[144,1024]{1,0:T(8,128)(2,1)} %bitcast.11, ...), custom_call_target="tpu_custom_call" | custom-call | flops 3400000000 | bytes 3000000 | tf_op jit(solution)/shard_map/hstu_backward/pallas_call | solution.py:462
  70.5 3.0 %finish.1 = (bf16[144,1024]{1,0:T(8,128)(2,1)}, bf16[144,1024]{1,0:T(8,128)(2,1)}, bf16[144,1024]{1,0:T(8,128)(2,1)}, bf16[144,1024]{1,0:T(8,128)(2,1)}) custom-call(s32[1,16]{1,0:T(1,128)} %tgt.3, bf16[8,144,128]{2,1,0:T(8,128)(2,1)} %get-tuple-element.12.q_ref, bf16[144,1024]{1,0:T(8,128)(2,1)} %get-tuple-element.13.k_ref, ...), custom_call_target="tpu_custom_call" | custom-call | tf_op jit(solution)/shard_map/finish/pallas_call | solution.py:496
